TPU v7x, 32 devices: a whole 2x2x4 slice. The times are simulated.
32 devices in a mesh: batch: 8 (over z, y), tm: 4 (over x, core).
Axes of the slice: x: 2, y: 2, z: 4, core: 2. Of those that a mesh axis runs over, the one named last changes fastest.
Arguments:
- patches: bfloat16 [32, 1024, 768], P('batch', 'tm'), may hold values from -6 to 6
- segment_ids: int32 [32, 1024], P('batch', 'tm'), may hold values from 0 to 4, as said below
- mask_flags: int32 [32, 1024], P('batch', 'tm'), may hold values 0 or 1
- cotangent: bfloat16 [32, 1024, 768], P('batch', 'tm'), may hold values from -6 to 6
- mask_embed: float32 [768], P(('batch', 'tm')), may hold values from -6 to 6
- norm_gain: float32 [2, 768], P(None, ('batch', 'tm')), may hold values from 0.1 to 1.9
- norm_shift: float32 [2, 768], P(None, ('batch', 'tm')), may hold values from -3 to 3
- qkv_weight: float32 [768, 2304], P(('batch', 'tm')), may hold values from -0.3125 to 0.3125
- qv_bias: float32 [2, 768], P(None, ('batch', 'tm')), may hold values from -3 to 3
- out_weight: float32 [768, 768], P(('batch', 'tm')), may hold values from -1.75 to 1.75
- branch_bias: float32 [2, 768], P(None, ('batch', 'tm')), may hold values from -3 to 3
- up_weight: float32 [768, 3072], P(('batch', 'tm')), may hold values from -0.21875 to 0.21875
- up_bias: float32 [3072], P(('batch', 'tm')), may hold values from -3 to 3
- down_weight: float32 [3072, 768], P(('batch', 'tm')), may hold values from -0.109375 to 0.109375
Outputs:
- output: float32 [32, 1024, 768], P('batch', 'tm')
- patch_grad: float32 [32, 1024, 768], P('batch', 'tm')
- mask_embed_grad: float32 [768], P(('batch', 'tm'))
- norm_gain_grad: float32 [2, 768], P(None, ('batch', 'tm'))
- norm_shift_grad: float32 [2, 768], P(None, ('batch', 'tm'))
- qkv_weight_grad: float32 [768, 2304], P(('batch', 'tm'))
- qv_bias_grad: float32 [2, 768], P(None, ('batch', 'tm'))
- out_weight_grad: float32 [768, 768], P(('batch', 'tm'))
- branch_bias_grad: float32 [2, 768], P(None, ('batch', 'tm'))
- up_weight_grad: float32 [768, 3072], P(('batch', 'tm'))
- up_bias_grad: float32 [3072], P(('batch', 'tm'))
- down_weight_grad: float32 [3072, 768], P(('batch', 'tm'))
Inputs may be any that keep to these rules, and one draw needn't show every extreme that they name: `segment_ids`: in each row the ids run 1, 2, 3, 4 in that order, the runs of 1 and 2 possibly empty, followed by 1 to 128 positions of id 0 (padding).
All inputs are finite; a program needn't handle non-finite values. No bound on the sum of `mask_flags` on one device may be relied on, other than what follows from the above.
Results may differ from a plain program's by a relative error of at most 0.017.
The roundings to bfloat16 on the way count: a program that leaves them out, or rounds other values in their place, can miss the bound.
Values may be sent and summed in bfloat16 or wider, within the bound.
A program may use at most 320 MiB of HBM per device.

v0:
```python
import math

import jax
import jax.numpy as jnp
from jax import lax
from jax.sharding import PartitionSpec as P

HEADS = 12


EPS = 1e-06
NEGATIVE = -1e30


def layer_norm(hidden, gain, shift):
    center = hidden - jnp.mean(hidden, -1, keepdims=True)
    spread = jnp.mean(center * center, -1, keepdims=True)
    return center * lax.rsqrt(spread + EPS) * gain + shift


def gelu_exact(values):
    return jax.nn.gelu(values, approximate=False)


def outer_sum(left, right):
    return lax.dot_general(
        left, right, (((0,), (0,)), ((), ())), preferred_element_type=jnp.float32
    )


def back_product(grad, weight):
    return lax.dot_general(
        grad, weight, (((1,), (1,)), ((), ())), preferred_element_type=jnp.float32
    )


def on_device(
    patches,
    segment_ids,
    mask_flags,
    cotangent,
    mask_embed,
    norm_gain,
    norm_shift,
    qkv_weight,
    qv_bias,
    out_weight,
    branch_bias,
    up_weight,
    up_bias,
    down_weight,
):
    rows, span, width = patches.shape
    head_dim = width // HEADS
    scale = 1.0 / math.sqrt(head_dim)
    count = rows * span
    block = min(rows, max(1, 512 // span))
    groups = rows // block
    (
        whole_embed,
        whole_gain,
        whole_shift,
        whole_qkv,
        whole_qvbias,
        whole_out,
        whole_bias,
        whole_up,
        whole_upbias,
        whole_down,
    ) = (
        lax.all_gather(mask_embed.astype(jnp.bfloat16), ("batch", "tm"), axis=0, tiled=True),
        lax.all_gather(norm_gain.astype(jnp.bfloat16), ("batch", "tm"), axis=1, tiled=True),
        lax.all_gather(norm_shift.astype(jnp.bfloat16), ("batch", "tm"), axis=1, tiled=True),
        lax.all_gather(qkv_weight.astype(jnp.bfloat16), ("batch", "tm"), axis=0, tiled=True),
        lax.all_gather(qv_bias.astype(jnp.bfloat16), ("batch", "tm"), axis=1, tiled=True),
        lax.all_gather(out_weight.astype(jnp.bfloat16), ("batch", "tm"), axis=0, tiled=True),
        lax.all_gather(branch_bias.astype(jnp.bfloat16), ("batch", "tm"), axis=1, tiled=True),
        lax.all_gather(up_weight.astype(jnp.bfloat16), ("batch", "tm"), axis=0, tiled=True),
        lax.all_gather(up_bias.astype(jnp.bfloat16), ("batch", "tm"), axis=0, tiled=True),
        lax.all_gather(down_weight.astype(jnp.bfloat16), ("batch", "tm"), axis=0, tiled=True),
    )
    gains = whole_gain.astype(jnp.float32)
    shifts = whole_shift.astype(jnp.float32)
    biases = whole_bias.astype(jnp.float32)
    qv_terms = whole_qvbias.astype(jnp.float32)
    masked = (mask_flags == 1)[..., None]
    start = jnp.where(masked, whole_embed.astype(jnp.float32), patches.astype(jnp.float32))
    first_in = layer_norm(start, gains[0], shifts[0]).astype(jnp.bfloat16).reshape(count, width)
    projected = jnp.dot(first_in, whole_qkv, preferred_element_type=jnp.float32)
    queries = (projected[:, :width] + qv_terms[0]).astype(jnp.bfloat16)
    keys_local = projected[:, width : 2 * width].astype(jnp.bfloat16)
    values_local = (projected[:, 2 * width :] + qv_terms[1]).astype(jnp.bfloat16)
    pairs = jnp.concatenate([keys_local, values_local], 1).reshape(rows, span, 2 * width)
    all_pairs, all_segments = (
        lax.all_gather(pairs, "tm", axis=1, tiled=True),
        lax.all_gather(segment_ids, "tm", axis=1, tiled=True),
    )
    total_keys = all_pairs.shape[1]
    query_blocks = queries.reshape(groups, block, span, width)
    pair_blocks = all_pairs.reshape(groups, block, total_keys, 2 * width)
    own_segments = segment_ids.reshape(groups, block, span)
    far_segments = all_segments.reshape(groups, block, total_keys)

    def masked_scores(query_blk, key_blk, query_seg, key_seg):
        lead = query_blk.shape[1]
        trail = key_blk.shape[1]
        query_heads = query_blk.reshape(block, lead, HEADS, head_dim)
        key_heads = key_blk.reshape(block, trail, HEADS, head_dim)
        scores = (
            jnp.einsum(
                "bqhd,bkhd->bhqk", query_heads, key_heads, preferred_element_type=jnp.float32
            )
            * scale
        )
        allowed = (query_seg[:, :, None] == key_seg[:, None, :])[:, None]
        return jnp.where(allowed, scores, NEGATIVE)

    def attend(items):
        query_blk, pair_blk, own_seg, far_seg = items
        scores = masked_scores(query_blk, pair_blk[..., :width], own_seg, far_seg)
        peak = jnp.max(scores, -1, keepdims=True)
        expon = jnp.exp(scores - peak)
        totals = jnp.sum(expon, -1, keepdims=True)
        probs_low = (expon / totals).astype(jnp.bfloat16)
        value_heads = pair_blk[..., width:].reshape(block, total_keys, HEADS, head_dim)
        mixed_blk = jnp.einsum(
            "bhqk,bkhd->bqhd", probs_low, value_heads, preferred_element_type=jnp.float32
        )
        return (mixed_blk.reshape(block, span, width), peak + jnp.log(totals))

    mixed, log_totals = lax.map(attend, (query_blocks, pair_blocks, own_segments, far_segments))
    mixed_low = mixed.reshape(count, width).astype(jnp.bfloat16)
    branch = jnp.dot(mixed_low, whole_out, preferred_element_type=jnp.float32) + biases[0]
    middle = start + branch.reshape(rows, span, width)
    second_in = layer_norm(middle, gains[1], shifts[1]).astype(jnp.bfloat16).reshape(count, width)
    hidden_pre = jnp.dot(
        second_in, whole_up, preferred_element_type=jnp.float32
    ) + whole_upbias.astype(jnp.float32)
    hidden_act = gelu_exact(hidden_pre).astype(jnp.bfloat16)
    result = jnp.dot(hidden_act, whole_down, preferred_element_type=jnp.float32) + biases[1]
    output = middle + result.reshape(rows, span, width)
    back_qkv, back_out, back_up, back_down = (
        lax.all_gather(qkv_weight.astype(jnp.bfloat16), ("batch", "tm"), axis=0, tiled=True),
        lax.all_gather(out_weight.astype(jnp.bfloat16), ("batch", "tm"), axis=0, tiled=True),
        lax.all_gather(up_weight.astype(jnp.bfloat16), ("batch", "tm"), axis=0, tiled=True),
        lax.all_gather(down_weight.astype(jnp.bfloat16), ("batch", "tm"), axis=0, tiled=True),
    )
    upstream = cotangent.astype(jnp.float32)
    result_grad = upstream.reshape(count, width).astype(jnp.bfloat16)
    down_bias_grad = jnp.sum(result_grad.astype(jnp.float32), 0)
    down_weight_grad = outer_sum(hidden_act, result_grad)
    act_grad = back_product(result_grad, back_down).astype(jnp.bfloat16)
    gelu_pull = jax.vjp(gelu_exact, hidden_pre)[1]
    pre_grad = gelu_pull(act_grad.astype(jnp.float32))[0].astype(jnp.bfloat16)
    up_bias_grad = jnp.sum(pre_grad.astype(jnp.float32), 0)
    up_weight_grad = outer_sum(second_in, pre_grad)
    second_grad = back_product(pre_grad, back_up).reshape(rows, span, width)
    norm_pull_two = jax.vjp(layer_norm, middle, gains[1], shifts[1])[1]
    middle_norm_grad, gain_two_grad, shift_two_grad = norm_pull_two(second_grad)
    middle_grad = upstream + middle_norm_grad
    branch_grad = middle_grad.reshape(count, width).astype(jnp.bfloat16)
    out_bias_grad = jnp.sum(branch_grad.astype(jnp.float32), 0)
    out_weight_grad = outer_sum(mixed_low, branch_grad)
    mixed_grad = back_product(branch_grad, back_out).astype(jnp.bfloat16)
    mixed_blocks = mixed_grad.reshape(groups, block, span, width)

    def query_back(items):
        query_blk, pair_blk, own_seg, far_seg, log_total, grad_blk = items
        scores = masked_scores(query_blk, pair_blk[..., :width], own_seg, far_seg)
        probs = jnp.exp(scores - log_total)
        probs_low = probs.astype(jnp.bfloat16)
        query_heads = query_blk.reshape(block, span, HEADS, head_dim)
        key_heads = pair_blk[..., :width].reshape(block, total_keys, HEADS, head_dim)
        value_heads = pair_blk[..., width:].reshape(block, total_keys, HEADS, head_dim)
        grad_heads = grad_blk.reshape(block, span, HEADS, head_dim)
        prob_grad = jnp.einsum(
            "bqhd,bkhd->bhqk", grad_heads, value_heads, preferred_element_type=jnp.float32
        )
        inner = jnp.sum(probs * prob_grad, -1, keepdims=True)
        score_grad = (probs * (prob_grad - inner)).astype(jnp.bfloat16)
        query_grad = (
            jnp.einsum("bhqk,bkhd->bqhd", score_grad, key_heads, preferred_element_type=jnp.float32)
            * scale
        )
        key_grad = (
            jnp.einsum(
                "bhqk,bqhd->bkhd", score_grad, query_heads, preferred_element_type=jnp.float32
            )
            * scale
        )
        value_grad = jnp.einsum(
            "bhqk,bqhd->bkhd", probs_low, grad_heads, preferred_element_type=jnp.float32
        )
        pair_grad = jnp.concatenate(
            [
                key_grad.reshape(block, total_keys, width),
                value_grad.reshape(block, total_keys, width),
            ],
            -1,
        )
        return (query_grad.reshape(block, span, width), pair_grad, inner)

    query_grads, pair_grads, unused_inner = lax.map(
        query_back,
        (query_blocks, pair_blocks, own_segments, far_segments, log_totals, mixed_blocks),
    )
    pair_grads = pair_grads.reshape(rows, total_keys, 2 * width)
    local_pair_grads = lax.psum_scatter(pair_grads, "tm", scatter_dimension=1, tiled=True).astype(
        jnp.bfloat16
    )
    query_low = query_grads.reshape(count, width).astype(jnp.bfloat16)
    local_pair_grads = local_pair_grads.reshape(count, 2 * width)
    qkv_grad = jnp.concatenate([query_low, local_pair_grads], 1)
    qkv_weight_grad = outer_sum(first_in, qkv_grad)
    qv_bias_grad = jnp.stack(
        [
            jnp.sum(query_low.astype(jnp.float32), 0),
            jnp.sum(local_pair_grads[:, width:].astype(jnp.float32), 0),
        ]
    )
    first_grad = back_product(qkv_grad, back_qkv).reshape(rows, span, width)
    norm_pull_one = jax.vjp(layer_norm, start, gains[0], shifts[0])[1]
    start_norm_grad, gain_one_grad, shift_one_grad = norm_pull_one(first_grad)
    start_grad = middle_grad + start_norm_grad
    embed_grad = jnp.sum(jnp.where(masked, start_grad, 0.0), (0, 1))
    patch_grad = jnp.where(masked, 0.0, start_grad)
    (
        embed_sum,
        gain_sum,
        shift_sum,
        qkv_sum,
        qv_sum,
        out_sum,
        branch_sum,
        up_sum,
        up_bias_sum,
        down_sum,
    ) = (
        lax.psum_scatter(embed_grad, ("batch", "tm"), scatter_dimension=0, tiled=True),
        lax.psum_scatter(
            jnp.stack([gain_one_grad, gain_two_grad]),
            ("batch", "tm"),
            scatter_dimension=1,
            tiled=True,
        ),
        lax.psum_scatter(
            jnp.stack([shift_one_grad, shift_two_grad]),
            ("batch", "tm"),
            scatter_dimension=1,
            tiled=True,
        ),
        lax.psum_scatter(qkv_weight_grad, ("batch", "tm"), scatter_dimension=0, tiled=True),
        lax.psum_scatter(qv_bias_grad, ("batch", "tm"), scatter_dimension=1, tiled=True),
        lax.psum_scatter(out_weight_grad, ("batch", "tm"), scatter_dimension=0, tiled=True),
        lax.psum_scatter(
            jnp.stack([out_bias_grad, down_bias_grad]),
            ("batch", "tm"),
            scatter_dimension=1,
            tiled=True,
        ),
        lax.psum_scatter(up_weight_grad, ("batch", "tm"), scatter_dimension=0, tiled=True),
        lax.psum_scatter(up_bias_grad, ("batch", "tm"), scatter_dimension=0, tiled=True),
        lax.psum_scatter(down_weight_grad, ("batch", "tm"), scatter_dimension=0, tiled=True),
    )
    return (
        output,
        patch_grad,
        embed_sum,
        gain_sum,
        shift_sum,
        qkv_sum,
        qv_sum,
        out_sum,
        branch_sum,
        up_sum,
        up_bias_sum,
        down_sum,
    )


def solution(mesh):
    return jax.shard_map(
        on_device,
        mesh=mesh,
        in_specs=(
            P("batch", "tm", None),
            P("batch", "tm"),
            P("batch", "tm"),
            P("batch", "tm", None),
            P(("batch", "tm")),
            P(None, ("batch", "tm")),
            P(None, ("batch", "tm")),
            P(("batch", "tm"), None),
            P(None, ("batch", "tm")),
            P(("batch", "tm"), None),
            P(None, ("batch", "tm")),
            P(("batch", "tm"), None),
            P(("batch", "tm")),
            P(("batch", "tm"), None),
        ),
        out_specs=(
            P("batch", "tm", None),
            P("batch", "tm", None),
            P(("batch", "tm")),
            P(None, ("batch", "tm")),
            P(None, ("batch", "tm")),
            P(("batch", "tm"), None),
            P(None, ("batch", "tm")),
            P(("batch", "tm"), None),
            P(None, ("batch", "tm")),
            P(("batch", "tm"), None),
            P(("batch", "tm")),
            P(("batch", "tm"), None),
        ),
        check_vma=False,
    )
```

profile of v0, /device:TPU:11, one launch (start us, length us, event | category | flops | bytes accessed | tf_op | source)
XLA Modules:
  0.0 1441.7 jit_solution(249910440686493078)
XLA Ops:
  10.7 39.6 %all-reduce.9 = (bf16[768]{0:T(1024)(128)(2,1)S(1)}, bf16[3072]{0:T(1024)(128)(2,1)S(1)}) all-reduce(bf16[768]{0:T(1024)(128)(2,1)S(1)} %dynamic-update-slice, bf16[3072]{0:T(1024)(128)(2,1)S(1)} %dynamic-update-slice.1), channel_id=1, replica_groups=mesh['batch'=8,'tm'=4] {'batch','tm'}, use_global_device_ids=true, to_apply=%add | all-reduce | flops 3840 | bytes 15360
  51.1 32.1 %all-gather = bf16[32,24,2]{1,2,0:T(2,128)(2,1)S(1)} all-gather(bf16[1,24,2]{1,2,0:T(2,128)(2,1)S(1)} %convert_bitcast_fusion.3), channel_id=1, replica_groups=mesh['batch'=8,'tm'=4] {'batch','tm'}, dimensions={0}, use_global_device_ids=true | all-gather | bytes 3168 | tf_op jit(solution)/shard_map/all_gather | solution.py:72
  84.2 39.7 %all-gather.1 = bf16[32,24,2]{1,2,0:T(2,128)(2,1)S(1)} all-gather(bf16[1,24,2]{1,2,0:T(2,128)(2,1)S(1)} %convert_bitcast_fusion.2), channel_id=1, replica_groups=mesh['batch'=8,'tm'=4] {'batch','tm'}, dimensions={0}, use_global_device_ids=true | all-gather | bytes 3168 | tf_op jit(solution)/shard_map/all_gather | solution.py:73
  124.8 36.4 %all-gather.2 = bf16[32,24,2]{1,2,0:T(2,128)(2,1)S(1)} all-gather(bf16[1,24,2]{1,2,0:T(2,128)(2,1)S(1)} %convert_bitcast_fusion.1), channel_id=1, replica_groups=mesh['batch'=8,'tm'=4] {'batch','tm'}, dimensions={0}, use_global_device_ids=true | all-gather | bytes 3168 | tf_op jit(solution)/shard_map/all_gather | solution.py:75
  185.6 37.8 %all-gather.3 = bf16[32,24,2]{1,2,0:T(2,128)(2,1)S(1)} all-gather(bf16[1,24,2]{1,2,0:T(2,128)(2,1)S(1)} %convert_bitcast_fusion), channel_id=1, replica_groups=mesh['batch'=8,'tm'=4] {'batch','tm'}, dimensions={0}, use_global_device_ids=true | all-gather | bytes 3168 | tf_op jit(solution)/shard_map/all_gather | solution.py:77
  227.1 35.9 %all-gather.12.cloned.1.call-done = bf16[4,1024,1536]{2,1,0:T(8,128)(2,1)} async-done(((bf16[4,256,1536]{2,1,0:T(8,128)(2,1)}), bf16[4,1024,1536]{2,1,0:T(8,128)(2,1)}) %all-gather.12.cloned.1.call-update) | async-done | bytes 12582928 | tf_op jit(solution)/shard_map/all_gather | solution.py:95
  263.0 16.6 %copy.58 = bf16[4,1024,1536]{1,2,0:T(8,128)(2,1)} copy(bf16[4,1024,1536]{2,1,0:T(8,128)(2,1)} %all-gather.12.cloned.1.call-done) | data formatting | bytes 25165824 | tf_op jit(solution)/shard_map/all_gather | solution.py:95
  280.9 80.3 %while.24 = (s32[]{:T(128)}, bf16[2,2,256,768]{3,2,1,0:T(8,128)(2,1)}, f32[2,2,12,256,1]{3,2,1,4,0:T(8,128)S(1)}, bf16[2,2,1024,1536]{2,3,1,0:T(8,128)(2,1)}, s3...) while((s32[]{:T(128)}, ...), condition=%wide.region_5.6_spmd, body=%wide.region_2.5_spmd.sunk | while | flops 1686628352 | bytes 115595880 | solution.py:131
  368.0 19.8 %all-gather.16.cloned.1.call-done = bf16[768,3072]{1,0:T(8,128)(2,1)} async-done(((bf16[24,3072]{1,0:T(8,128)(2,1)}), bf16[768,3072]{1,0:T(8,128)(2,1)}) %all-gather.16.cloned.1.call-update) | async-done | bytes 4718608 | tf_op jit(solution)/shard_map/all_gather | solution.py:78
  387.8 36.2 %multiply_convert_fusion.1 = (bf16[1024,3072]{1,0:T(8,128)(2,1)}, f32[1024,3072]{1,0:T(8,128)}, f32[1024,3072]{1,0:T(8,128)}) fusion(f32[3072]{0:T(1024)S(1)} %copy-done.62, bf16[1024,768]{1,0:T(8,128)(2,1)S(1)} %bitcast.227, bf16[768,3072]{1,0:T(8,128)(2,1)} %all-gather.16.cloned.1.call-done), kind=kOutput, calls=%fused_computation.48 | convolution fusion | flops 5039456256 | bytes 37761024 | tf_op jit(solution)/shard_map/dot_general | solution.py:136
  423.9 29.6 %all-gather.18.cloned.1.call-done = bf16[3072,768]{1,0:T(8,128)(2,1)} async-done(((bf16[96,768]{1,0:T(8,128)(2,1)}), bf16[3072,768]{1,0:T(8,128)(2,1)}) %all-gather.18.cloned.1.call-update) | async-done | bytes 4718608 | tf_op jit(solution)/shard_map/all_gather | solution.py:80
  453.6 17.3 %convert_reduce_fusion = (f32[3072]{0:T(1024)}, bf16[1024,3072]{1,0:T(8,128)(2,1)}) fusion(f32[1024,3072]{1,0:T(8,128)} %get-tuple-element.223, bf16[1024,768]{1,0:T(8,128)(2,1)S(1)} %bitcast.216, bf16[3072,768]{1,0:T(8,128)(2,1)} %all-gather.18.cloned.1.call-done, f32[1024,3072]{1,0:T(8,128)} %get-tuple-element.239, f32[3072]{0:T(1024)S(1)} %copy-done.62), kind=kOutput, calls=%fused_computation.47 | convolution fusion | flops 4891603968 | bytes 37773312 | tf_op jit(solution)/shard_map/dot_general | solution.py:32
  497.9 246.7 %while.25 = (s32[]{:T(128)}, bf16[2,2,256,768]{3,2,1,0:T(8,128)(2,1)}, f32[2,2,1024,1536]{3,2,1,0:T(8,128)}, bf16[2,2,1024,1536]{2,3,1,0:T(8,128)(2,1)}, s32[2,2...) while((s32[]{:T(128)}, ...), condition=%wide.region_12.13_spmd, body=%wide.region_10.12_spmd.sunk | while | flops 4126926848 | bytes 399973696 | solution.py:203
  518.5 19.4 %multiply_reduce_fusion.8 = (f32[2,12,256]{2,1,0:T(8,128)S(1)}, f32[2,12,256,1024]{3,2,1,0:T(8,128)}) fusion(f32[2,12,256,1024]{3,2,1,0:T(8,128)} %fusion.125, f32[2,12,256]{2,1,0:T(8,128)S(1)} %dynamic-slice_bitcast_fusion.16, pred[2,256,1024]{2,1,0:T(8,128)(4,1)} %broadcast_compare_fusion.6, bf16[2,256,12,64]{1,3,2,0:T(8,128)(2,1)} %bitcast.204, ...), kind=kOutput, calls=%fused_computation.16.clone.1 | convolution fusion | flops 836757504 | bytes 54837248 | tf_op jit(solution)/shard_map/while/body/eval_jaxpr/bqhd,bkhd->bhqk/dot_general | solution.py:176
  538.0 17.0 %multiply_convert_fusion.3 = bf16[2,12,256,1024]{3,2,1,0:T(8,128)(2,1)S(1)} fusion(f32[2,12,256,1024]{3,2,1,0:T(8,128)} %get-tuple-element.362, f32[2,12,256,1024]{3,2,1,0:T(8,128)} %fusion.125, f32[2,12,256]{2,1,0:T(8,128)S(1)} %get-tuple-element.363, f32[2,12,256]{2,1,0:T(8,128)S(1)} %dynamic-slice_bitcast_fusion.16, ...), kind=kLoop, calls=%fused_computation.15.clone.1 | loop fusion | flops 37748736 | bytes 63488000 | tf_op jit(solution)/shard_map/while/body/eval_jaxpr/convert_element_type | solution.py:180
  561.5 12.9 fusion.127
  641.6 19.4 %multiply_reduce_fusion.8 = (f32[2,12,256]{2,1,0:T(8,128)S(1)}, f32[2,12,256,1024]{3,2,1,0:T(8,128)}) fusion(f32[2,12,256,1024]{3,2,1,0:T(8,128)} %fusion.125, f32[2,12,256]{2,1,0:T(8,128)S(1)} %dynamic-slice_bitcast_fusion.16, pred[2,256,1024]{2,1,0:T(8,128)(4,1)} %broadcast_compare_fusion.6, bf16[2,256,12,64]{1,3,2,0:T(8,128)(2,1)} %bitcast.204, ...), kind=kOutput, calls=%fused_computation.16.clone.1 | convolution fusion | flops 836757504 | bytes 54837248 | tf_op jit(solution)/shard_map/while/body/eval_jaxpr/bqhd,bkhd->bhqk/dot_general | solution.py:176
  661.1 17.0 %multiply_convert_fusion.3 = bf16[2,12,256,1024]{3,2,1,0:T(8,128)(2,1)S(1)} fusion(f32[2,12,256,1024]{3,2,1,0:T(8,128)} %get-tuple-element.362, f32[2,12,256,1024]{3,2,1,0:T(8,128)} %fusion.125, f32[2,12,256]{2,1,0:T(8,128)S(1)} %get-tuple-element.363, f32[2,12,256]{2,1,0:T(8,128)S(1)} %dynamic-slice_bitcast_fusion.16, ...), kind=kLoop, calls=%fused_computation.15.clone.1 | loop fusion | flops 37748736 | bytes 63488000 | tf_op jit(solution)/shard_map/while/body/eval_jaxpr/convert_element_type | solution.py:180
  776.6 145.7 %reduce-scatter.10.cloned.1.call-done = f32[4,256,1536]{2,1,0:T(8,128)} async-done(((f32[4,1024,1536]{2,1,0:T(8,128)}), f32[4,256,1536]{2,1,0:T(8,128)}) %reduce-scatter.10.cloned.1.call-update) | async-done | bytes 6291472 | tf_op jit(solution)/shard_map/reduce_scatter | solution.py:208
  950.5 41.2 %all-reduce.8 = (f32[768]{0:T(1024)S(1)}, f32[2,768]{1,0:T(2,128)S(1)}, f32[2,768]{1,0:T(2,128)S(1)}, f32[2,768]{1,0:T(2,128)S(1)}, f32[2,768]{1,0:T(2,128)S(1)}, /*index=5*/f32[3072]{0:T(1024)S(1)}) all-reduce(f32[768]{0:T(1024)S(1)} %get-tuple-element.220, ...), channel_id=3, replica_groups=mesh['batch'=8,'tm'=4] {'batch','tm'}, use_global_device_ids=true, to_apply=%region_17.18.clone | all-reduce | flops 9984 | bytes 79872
  996.1 31.2 %reduce-scatter.14.cloned.1.call-done = f32[24,768]{1,0:T(8,128)} async-done(((f32[768,768]{1,0:T(8,128)}), f32[24,768]{1,0:T(8,128)}) %reduce-scatter.14.cloned.1.call-update) | async-done | bytes 73744 | tf_op jit(solution)/shard_map/reduce_scatter | solution.py:254
  1027.3 140.8 %reduce-scatter.16.cloned.1.call-done = f32[24,3072]{1,0:T(8,128)} async-done(((f32[768,3072]{1,0:T(8,128)}), f32[24,3072]{1,0:T(8,128)}) %reduce-scatter.16.cloned.1.call-update) | async-done | bytes 294928 | tf_op jit(solution)/shard_map/reduce_scatter | solution.py:261
  1168.0 142.1 %reduce-scatter.18.cloned.1.call-done = f32[96,768]{1,0:T(8,128)} async-done(((f32[3072,768]{1,0:T(8,128)}), f32[96,768]{1,0:T(8,128)}) %reduce-scatter.18.cloned.1.call-update) | async-done | bytes 294928 | tf_op jit(solution)/shard_map/reduce_scatter | solution.py:263
  1310.1 124.5 %reduce-scatter.12.cloned.1.call-done = f32[24,2304]{1,0:T(8,128)} async-done(((f32[768,2304]{1,0:T(8,128)}), f32[24,2304]{1,0:T(8,128)}) %reduce-scatter.12.cloned.1.call-update) | async-done | bytes 221200 | tf_op jit(solution)/shard_map/reduce_scatter | solution.py:252
  (332 shorter events, 373.1 us)
Async XLA Ops:
  7.2 158.2 %copy-start.7 = (bf16[4,256,768]{2,1,0:T(8,128)(2,1)S(1)}, bf16[4,256,768]{2,1,0:T(8,128)(2,1)}, u32[]{:S(2)}) copy-start(bf16[4,256,768]{2,1,0:T(8,128)(2,1)} %param.18) | copy-start | bytes 4718596
  7.2 160.5 %all-gather.10.cloned.1.call-start = ((), (), s32[]{:S(2)}) async-start(), calls=%async_computation.5 | async-start | bytes 3649536 | tf_op jit(solution)/shard_map/all_gather | solution.py:74
  9.0 254.0 %all-gather.12.cloned.1.call-start = ((), (), s32[]{:S(2)}) async-start(), calls=%async_computation.6 | async-start | bytes 15728640 | tf_op jit(solution)/shard_map/all_gather | solution.py:95
  50.4 123.7 %copy-start.31 = (f32[768]{0:T(1024)}, f32[768]{0:T(1024)S(1)}, u32[]{:S(2)}) copy-start(f32[768]{0:T(1024)S(1)} %convert_element_type.142) | copy-start | bytes 9220
  178.0 183.2 %all-gather.14.cloned.1.call-start = ((), (), s32[]{:S(2)}) async-start(), calls=%async_computation.7 | async-start | bytes 1216512 | tf_op jit(solution)/shard_map/all_gather | solution.py:76
  178.7 209.0 %all-gather.16.cloned.1.call-start = ((), (), s32[]{:S(2)}) async-start(), calls=%async_computation.8 | async-start | bytes 4866048 | tf_op jit(solution)/shard_map/all_gather | solution.py:78
  179.5 274.1 %all-gather.18.cloned.1.call-start = ((), (), s32[]{:S(2)}) async-start(), calls=%async_computation.9 | async-start | bytes 4866048 | tf_op jit(solution)/shard_map/all_gather | solution.py:80
  180.3 742.0 %reduce-scatter.10.cloned.1.call-start = ((), (), s32[]{:S(2)}) async-start(), calls=%async_computation.10 | async-start | bytes 31457280 | tf_op jit(solution)/shard_map/reduce_scatter | solution.py:208
  280.9 80.3 %copy-start.65 = (f32[768]{0:T(1024)S(1)}, f32[768]{0:T(1024)}, u32[]{:S(2)}) copy-start(f32[768]{0:T(1024)} %get-tuple-element.171) | copy-start | bytes 9220
  365.7 22.0 %copy-start.62 = (f32[3072]{0:T(1024)S(1)}, f32[3072]{0:T(1024)}, u32[]{:S(2)}) copy-start(f32[3072]{0:T(1024)} %convert_element_type.162) | copy-start | bytes 36868
  367.9 56.0 %copy-start.22 = (bf16[4,256,768]{2,1,0:T(8,128)(2,1)}, bf16[4,256,768]{2,1,0:T(8,128)(2,1)S(1)}, u32[]{:S(2)}) copy-start(bf16[4,256,768]{2,1,0:T(8,128)(2,1)S(1)} %add_convert_fusion) | copy-start | bytes 4718596
  387.8 65.8 %copy-start.17 = (bf16[4,256,768]{2,1,0:T(8,128)(2,1)S(1)}, bf16[4,256,768]{2,1,0:T(8,128)(2,1)}, u32[]{:S(2)}) copy-start(bf16[4,256,768]{2,1,0:T(8,128)(2,1)} %param.21) | copy-start | bytes 4718596
  470.9 11.5 copy-start.70
  504.0 10.1 copy-start.1
  504.0 11.3 copy-start.14
  538.0 17.0 %copy-start.2 = (bf16[1,2,256,768]{2,3,1,0:T(8,128)(2,1)S(1)}, bf16[1,2,256,768]{2,3,1,0:T(8,128)(2,1)}, u32[]{:S(2)}) copy-start(bf16[1,2,256,768]{2,3,1,0:T(8,128)(2,1)} %copy-done.1) | copy-start | bytes 2359300 | tf_op jit(solution)/shard_map/while
  627.1 10.1 copy-start.1
  627.1 11.3 copy-start.14
  661.1 17.0 %copy-start.2 = (bf16[1,2,256,768]{2,3,1,0:T(8,128)(2,1)S(1)}, bf16[1,2,256,768]{2,3,1,0:T(8,128)(2,1)}, u32[]{:S(2)}) copy-start(bf16[1,2,256,768]{2,3,1,0:T(8,128)(2,1)} %copy-done.1) | copy-start | bytes 2359300 | tf_op jit(solution)/shard_map/while
  744.6 282.6 %reduce-scatter.14.cloned.1.call-start = ((), (), s32[]{:S(2)}) async-start(), calls=%async_computation.12 | async-start | bytes 2433024 | tf_op jit(solution)/shard_map/reduce_scatter | solution.py:254
  750.2 417.8 %reduce-scatter.16.cloned.1.call-start = ((), (), s32[]{:S(2)}) async-start(), calls=%async_computation.13 | async-start | bytes 9732096 | tf_op jit(solution)/shard_map/reduce_scatter | solution.py:261
  762.9 547.3 %reduce-scatter.18.cloned.1.call-start = ((), (), s32[]{:S(2)}) async-start(), calls=%async_computation.14 | async-start | bytes 9732096 | tf_op jit(solution)/shard_map/reduce_scatter | solution.py:263
  776.4 658.3 %reduce-scatter.12.cloned.1.call-start = ((), (), s32[]{:S(2)}) async-start(), calls=%async_computation.11 | async-start | bytes 7299072 | tf_op jit(solution)/shard_map/reduce_scatter | solution.py:252
  925.5 12.2 copy-start.15
  (64 other events, 249.5 us)
Sparse Core Ops, SparseCore 0:
  11.5 61.1 all-gather.9
  178.1 84.8 all-gather.11
  266.5 54.0 all-gather.13
  323.9 63.8 all-gather.15
  391.1 62.4 all-gather.17
  744.7 177.5 reduce-scatter.9
  929.0 98.2 reduce-scatter.13
  1033.7 134.2 reduce-scatter.15
  1175.5 134.5 reduce-scatter.17
  1316.2 118.3 reduce-scatter.11
where the time goes:
time: 1450 us; the launch traced here: 1440 us
  waiting for transfers between devices  670 us (46%)
  matrix products  285 us (20%)
  blocking collectives  232 us (16%)
  other arithmetic  121 us (8%)
  local copies, waits for them, and re-layouts  117 us (8%)
  between operations  15.2 us (1%)
    reduce_scatter x1, waiting for transfers between devices, on_device(): lax.psum_scatter(pair_grads, 'tm', scatter_dimension=1, tiled=True)  146 us
    reduce_scatter x1, waiting for transfers between devices, on_device(): lax.psum_scatter(down_weight_grad, ('batch', 'tm'), scatter_dimension=0,...  142 us
    reduce_scatter x1, waiting for transfers between devices, on_device(): lax.psum_scatter(up_weight_grad, ('batch', 'tm'), scatter_dimension=0, ti...  141 us
    reduce_scatter x1, waiting for transfers between devices, on_device(): lax.psum_scatter(qkv_weight_grad, ('batch', 'tm'), scatter_dimension=0, t...  125 us
    unnamed x2, blocking collectives  80.8 us
    dynamic_update_slice x4, local copies, waits for them, and re-layouts, on_device(): lax.map(query_back, (query_blocks, pair_blocks, own_segments, far_segment...  46.1 us
    dot_general x4, matrix products, masked_scores(): jnp.einsum('bqhd,bkhd->bhqk', query_heads, key_heads, preferred_element_t...  41.5 us
    all_gather x1, blocking collectives, on_device(): lax.all_gather(norm_shift.astype(jnp.bfloat16), ('batch', 'tm'), axis=1,...  39.7 us
  transfers between devices with their start and end apart: 10, of which 8 were waited for; matrix products, arithmetic and copies ran while one was open for 15% of the time, Pallas kernels for 0%

commit v1 on v0

--- a/solution.py
+++ b/solution.py
@@ -1,15 +1,1220 @@
+import functools
 import math
 
 import jax
 import jax.numpy as jnp
 from jax import lax
+from jax.experimental import pallas as pl
+from jax.experimental.pallas import tpu as pltpu
 from jax.sharding import PartitionSpec as P
 
 HEADS = 12
-
-
 EPS = 1e-06
-NEGATIVE = -1e30
+FAR = -1e30
+LOG2E = math.log2(math.e)
+BF = jnp.bfloat16
+F32 = jnp.float32
+MESH = pl.DeviceIdType.MESH
+HBM = pl.BlockSpec(memory_space=pl.ANY)
+SLOPE = 0.36
+TAIL = (
+    0.14371305209487725,
+    0.14177235930704382,
+    0.1397197719471602,
+    0.026547986328787306,
+    0.18095585464885458,
+    -0.1797659534284226,
+    0.04705662553510592,
+)
+
+
+def nn(left, right):
+    return jnp.dot(left, right, preferred_element_type=F32)
+
+
+def nt(left, right):
+    return lax.dot_general(left, right, (((1,), (1,)), ((), ())), preferred_element_type=F32)
+
+
+def tn(left, right):
+    return lax.dot_general(left, right, (((0,), (0,)), ((), ())), preferred_element_type=F32)
+
+
+def gelu_and_slope(pre):
+    size = jnp.abs(pre)
+    t = 1.0 / (1.0 + SLOPE * size)
+    poly = jnp.full_like(t, TAIL[-1])
+    for term in TAIL[-2::-1]:
+        poly = poly * t + term
+    bell = jnp.exp2(pre * pre * (-0.5 * LOG2E))
+    lower = poly * t * bell
+    cdf = jnp.where(pre >= 0, 1.0 - lower, lower)
+    return pre * cdf, cdf + pre * bell * (1.0 / math.sqrt(2.0 * math.pi))
+
+
+def moments(hidden):
+    center = hidden - jnp.mean(hidden, -1, keepdims=True)
+    return center, lax.rsqrt(jnp.mean(center * center, -1, keepdims=True) + EPS)
+
+
+def norm_back(normed, rate, gain, grad):
+    scaled = grad * gain
+    shared = jnp.mean(scaled * normed, -1, keepdims=True)
+    return rate * (scaled - jnp.mean(scaled, -1, keepdims=True) - normed * shared)
+
+
+def column_sum(values):
+    return jnp.sum(values, 0, keepdims=True)
+
+
+class Place:
+    def __init__(self, deep):
+        batch, tm = lax.axis_index("batch"), lax.axis_index("tm")
+        self.deep = deep
+        self.batch, self.tm = batch, tm
+        self.z, self.y = batch // 2, batch % 2
+        self.x, self.c = tm // 2, tm % 2
+
+    def device(self, z=None, y=None, x=None, c=None):
+        z = self.z if z is None else z
+        y = self.y if y is None else y
+        x = self.x if x is None else x
+        c = self.c if c is None else c
+        return (z * 2 + y, x * 2 + c)
+
+    def mate(self, k):
+        return (self.x + k // 2) % 2 * 2 + (self.c + k % 2) % 2
+
+    def enter(self):
+        barrier = pltpu.get_barrier_semaphore()
+        others = [self.device(c=1 - self.c), self.device(x=1 - self.x), self.device(y=1 - self.y)]
+        others.append(self.device(x=1 - self.x, c=1 - self.c))
+        others += [self.device(z=(self.z + d) % self.deep) for d in range(1, self.deep)]
+        for other in others:
+            pl.semaphore_signal(barrier, inc=1, device_id=other, device_id_type=MESH)
+        pl.semaphore_wait(barrier, len(others))
+
+
+def remote(src, dst, send, recv, device):
+    return pltpu.make_async_remote_copy(
+        src_ref=src, dst_ref=dst, send_sem=send, recv_sem=recv, device_id=device, device_id_type=MESH
+    )
+
+
+class Route:
+    def __init__(self, place, order, crossed):
+        self.place, self.order, self.crossed = place, order, crossed
+        c = place.c
+        self.own = {
+            "z": place.z,
+            "p": c * place.y + (1 - c) * place.x if crossed else place.x,
+            "q": c * place.x + (1 - c) * place.y if crossed else place.y,
+        }
+        self.size = {"z": place.deep, "p": 2, "q": 2}
+        self.sizes = [self.size[axis] for axis in order]
+
+    def shifted(self, shifts):
+        at = {a: (self.own[a] + s % self.size[a]) % self.size[a] for a, s in zip(self.order, shifts)}
+        c = self.place.c
+        if self.crossed:
+            return at["z"], c * at["p"] + (1 - c) * at["q"], c * at["q"] + (1 - c) * at["p"]
+        return at["z"], at["q"], at["p"]
+
+    def device(self, shifts):
+        z, y, x = self.shifted(shifts)
+        return self.place.device(z=z, y=y, x=x)
+
+    def chip(self, shifts):
+        z, y, x = self.shifted(shifts)
+        return (z * 2 + y) * 2 + x
+
+    def offsets(self, upto):
+        found = [()]
+        for stage, size in enumerate(self.sizes):
+            found = [f + (o,) for f in found for o in range(size if stage < upto else 1)]
+        return found
+
+    def index(self, offset):
+        flat = 0
+        for o, size in zip(offset, self.sizes):
+            flat = flat * size + o
+        return flat
+
+
+class Gather:
+    def __init__(self, place, route, shard, joined, full, local, sends, recvs):
+        self.place, self.route = place, route
+        self.shard, self.joined, self.full = shard, joined, full
+        self.local, self.sends, self.recvs = local, sends, recvs
+        self.rows = shard.shape[0]
+        self.half = shard.shape[1] // 2
+        self.sent = []
+        self.count = 0
+
+    def columns(self, c):
+        return pl.ds(pl.multiple_of(c * self.half, 128), self.half)
+
+    def region(self, chip, c):
+        rows = 2 * self.rows
+        return self.full.at[pl.ds(pl.multiple_of(chip * rows, 16), rows), self.columns(c)]
+
+    def ship(self, src, dst, recv, device):
+        copy = remote(src, dst, self.sends.at[self.count], recv, device)
+        copy.start()
+        self.count += 1
+        self.sent.append(copy)
+
+    def join(self):
+        place = self.place
+        own = pl.ds(pl.multiple_of(place.c * self.rows, 8), self.rows)
+        self.mine = pltpu.make_async_copy(
+            self.shard.at[:, self.columns(place.c)], self.joined.at[own], self.local
+        )
+        self.mine.start()
+        self.pair = self.recvs.at[0]
+        self.ship(
+            self.shard.at[:, self.columns(1 - place.c)],
+            self.joined.at[own],
+            self.recvs.at[0],
+            place.device(c=1 - place.c),
+        )
+
+    def arrive(self, offset, stage):
+        route, place = self.route, self.place
+        chip = route.chip([-o for o in offset])
+        block = self.region(chip, place.c)
+        for later in range(stage + 1, 3):
+            for d in range(1, route.sizes[later]):
+                shifts = [0, 0, 0]
+                shifts[later] = d
+                seen = list(offset)
+                seen[later] = d
+                self.ship(block, block, self.recvs.at[1 + route.index(seen)], route.device(shifts))
+        total = math.prod(route.sizes)
+        self.ship(
+            block,
+            block,
+            self.recvs.at[1 + total + route.index(offset)],
+            place.device(c=1 - place.c),
+        )
+
+    def first(self):
+        place = self.place
+        self.mine.wait()
+        own = pl.ds(pl.multiple_of((1 - place.c) * self.rows, 8), self.rows)
+        self.sent[0].wait_send()
+        remote(
+            self.joined.at[own], self.joined.at[own], self.sends.at[0], self.recvs.at[0], place.device(c=1 - place.c)
+        ).wait_recv()
+        chip = self.route.chip([0, 0, 0])
+        self.region(chip, place.c)[...] = self.joined[...].astype(BF)
+        self.arrive((0, 0, 0), -1)
+
+    def stage(self, stage):
+        route = self.route
+        for offset in route.offsets(stage + 1):
+            if offset[stage] == 0:
+                continue
+            block = self.region(route.chip([-o for o in offset]), self.place.c)
+            remote(
+                block, block, self.sends.at[0], self.recvs.at[1 + route.index(offset)], self.place.device()
+            ).wait_recv()
+            self.arrive(offset, stage)
+
+    def finish(self):
+        route = self.route
+        total = math.prod(route.sizes)
+        for offset in route.offsets(3):
+            block = self.region(route.chip([-o for o in offset]), 1 - self.place.c)
+            remote(
+                block,
+                block,
+                self.sends.at[0],
+                self.recvs.at[1 + total + route.index(offset)],
+                self.place.device(),
+            ).wait_recv()
+
+    def drain(self):
+        for copy in self.sent[1:]:
+            copy.wait_send()
+
+
+def sum_vectors(place, held, slots, sends, recvs):
+    stages = [
+        [place.device(c=1 - place.c)],
+        [place.device(x=1 - place.x)],
+        [place.device(y=1 - place.y)],
+        [place.device(z=(place.z + d) % place.deep) for d in range(1, place.deep)],
+    ]
+    slot = 0
+    for stage, others in enumerate(stages):
+        copies = []
+        for other in others:
+            copies.append(remote(held.at[stage], slots.at[slot], sends.at[slot], recvs.at[slot], other))
+            copies[-1].start()
+            slot += 1
+        total = held[stage]
+        for copy in copies:
+            copy.wait()
+        for back in range(len(others)):
+            total = total + slots[slot - len(others) + back]
+        held[stage + 1] = total
+
+
+def code_columns(code, source):
+    turned = jnp.transpose(code[source])
+    flags = jnp.concatenate([turned[:, 0:1], turned[:, 1:2]], 0)
+    clips = jnp.concatenate([turned[:, 2:3], turned[:, 3:4]], 0)
+    return flags, clips
+
+
+def forward_kernel(
+    deep,
+    patches,
+    cotangent,
+    code_in,
+    small_in,
+    shard_qkv,
+    shard_out,
+    shard_up,
+    shard_down,
+    o_qkv,
+    o_out,
+    o_up,
+    o_down,
+    o_small,
+    o_x,
+    o_cot,
+    o_code,
+    o_first,
+    o_q,
+    o_k,
+    o_v,
+    o_mixed,
+    o_second,
+    o_rate,
+    o_middle,
+    o_act,
+    o_slope,
+    o_expon,
+    o_result,
+    w_qkv,
+    w_out,
+    w_up,
+    w_down,
+    j_qkv,
+    j_out,
+    j_up,
+    j_down,
+    small,
+    small_slots,
+    x,
+    code,
+    first,
+    q,
+    k,
+    v,
+    mixed,
+    second,
+    rate,
+    middle,
+    expon,
+    act,
+    slope,
+    result,
+    q_code,
+    k_code,
+    join_sems,
+    gather_sends,
+    gather_recvs,
+    small_sends,
+    small_recvs,
+    row_sends,
+    row_recvs,
+    local_sems,
+    expon_sems,
+    act_sems,
+):
+    place = Place(deep)
+    span, width = patches.shape[1:]
+    rows = x.shape[0]
+    sources = rows // span
+    half = width // HEADS
+    pairs = HEADS // 2
+    inner = w_up.shape[1]
+    chunks = inner // width
+
+    near = pltpu.make_async_copy(small_in, small.at[0], local_sems.at[0])
+    near.start()
+    place.enter()
+
+    kinds = ((patches, x), (code_in, code), (cotangent, o_cot))
+
+    def own_part(kind):
+        src, dst = kinds[kind]
+        to = dst.at[pl.ds(pl.multiple_of(place.tm * span, span), span)] if kind != 1 else dst.at[place.tm]
+        return pltpu.make_async_copy(src.at[place.tm], to, local_sems.at[1 + kind])
+
+    def row_copy(kind, step, to):
+        src, dst = kinds[kind]
+        here = dst.at[pl.ds(pl.multiple_of(place.tm * span, span), span)] if kind != 1 else dst.at[place.tm]
+        return remote(
+            src.at[to], here, row_sends.at[kind, step], row_recvs.at[kind, step], (place.batch, to)
+        )
+
+    def row_wait(kind, step):
+        src, dst = kinds[kind]
+        source = place.mate(step)
+        there = dst.at[pl.ds(pl.multiple_of(source * span, span), span)] if kind != 1 else dst.at[source]
+        remote(
+            there, there, row_sends.at[kind, step], row_recvs.at[kind, step], (place.batch, source)
+        ).wait_recv()
+
+    zpq = Route(place, "zpq", True)
+    pzq = Route(place, "pzq", False)
+    gathers = [
+        Gather(place, route, shard, joined, full, join_sems.at[i], gather_sends.at[i], gather_recvs.at[i])
+        for i, (route, shard, joined, full) in enumerate(
+            (
+                (zpq, shard_qkv, j_qkv, w_qkv),
+                (zpq, shard_out, j_out, w_out),
+                (zpq, shard_up, j_up, w_up),
+                (pzq, shard_down, j_down, w_down),
+            )
+        )
+    ]
+    for gather in gathers:
+        gather.join()
+    gathers[0].first()
+    for kind in (1, 0):
+        own_part(kind).start()
+        for step in range(1, sources):
+            row_copy(kind, step, place.mate(step)).start()
+    near.wait()
+    sum_vectors(place, small, small_slots, small_sends, small_recvs)
+    gathers[0].stage(0)
+    gathers[0].stage(1)
+    for gather in gathers[1:]:
+        gather.first()
+    own_part(2).start()
+    for step in range(1, sources):
+        row_copy(2, step, place.mate(step)).start()
+    gathers[0].stage(2)
+    gathers[0].finish()
+
+    vectors = small.at[4]
+    lane = lax.broadcasted_iota(jnp.int32, (1, 2 * half), 1)
+    low = lane < half
+    own_lanes = [low.astype(F32), 1.0 - low.astype(F32)]
+
+    for kind in (1, 0):
+        own_part(kind).wait()
+
+    @pl.loop(0, sources)
+    def _(step):
+        @pl.when(step > 0)
+        def _():
+            row_wait(1, step)
+            row_wait(0, step)
+
+        source = place.mate(step)
+        at = pl.ds(pl.multiple_of(source * span, span), span)
+        flags, clips = code_columns(code, source)
+        start = jnp.where(flags == 1.0, vectors[0:1, :], x[at, :].astype(F32))
+        middle[at, :] = start
+        center, speed = moments(start)
+        normed = (center * speed * vectors[1:2, :] + vectors[3:4, :]).astype(BF)
+        first[at, :] = normed
+        q[at, :] = (nn(normed, w_qkv[:, 0:width]) + vectors[5:6, :]).astype(BF) * (1.0 / math.sqrt(half))
+        k[at, :] = nn(normed, w_qkv[:, width : 2 * width]).astype(BF)
+        v[at, :] = (nn(normed, w_qkv[:, 2 * width :]) + vectors[6:7, :]).astype(BF)
+        clip_lane = lax.broadcasted_iota(jnp.int32, (span, 2 * half), 1).astype(F32)
+        for h in range(2):
+            base = float(half * (1 - h))
+            same = clip_lane - base == clips
+            named = jnp.logical_and(clip_lane >= base, clip_lane < base + 5.0)
+            q_code[h, at, :] = jnp.where(same, 1.0, 0.0).astype(BF)
+            k_code[h, at, :] = jnp.where(jnp.logical_and(named, jnp.logical_not(same)), FAR, 0.0).astype(BF)
+
+    for gather in gathers[1:]:
+        gather.stage(0)
+    block = min(rows, 512)
+
+    def expon_copy(p):
+        return pltpu.make_async_copy(expon.at[p % 2], o_expon.at[pl.ds(2 * p, 2)], expon_sems.at[p % 2])
+
+    def attend(p):
+        lanes = pl.ds(pl.multiple_of(p * 2 * half, 128), 2 * half)
+
+        @pl.when(p >= 2)
+        def _():
+            expon_copy(p - 2).wait()
+
+        slot = p % 2
+        keys, values = [], []
+        for h in range(2):
+            mask = own_lanes[h].astype(BF)
+            keys.append(k[:, lanes] * mask + k_code[h])
+            values.append(v[:, lanes] * mask + own_lanes[1 - h].astype(BF))
+        for part in range(rows // block):
+            at = pl.ds(part * block, block)
+            mixes = []
+            for h in range(2):
+                query = q[at, lanes] * own_lanes[h].astype(BF) + q_code[h, at, :]
+                scores = nt(query, keys[h])
+                peak = jnp.max(scores, -1, keepdims=True)
+                weights = jnp.exp2((scores - peak) * LOG2E).astype(BF)
+                expon[slot, h, at, :] = weights
+                mixes.append(nn(weights, values[h]))
+            top = jnp.where(low, mixes[0], mixes[1])
+            totals = pltpu.roll(jnp.where(low, mixes[1], mixes[0]), half, 1)
+            speed = 1.0 / totals
+            rate[at, lanes] = speed
+            mixed[at, lanes] = (top * speed).astype(BF)
+        expon_copy(p).start()
+
+    pl.loop(0, pairs)(attend)
+    for stage in (1, 2):
+        for gather in gathers[1:]:
+            gather.stage(stage)
+    for gather in gathers[1:]:
+        gather.finish()
+
+    def act_copies(step, j, at):
+        slot = step % 2
+        return (
+            pltpu.make_async_copy(act.at[slot, j], o_act.at[j, at], act_sems.at[0, slot, j]),
+            pltpu.make_async_copy(slope.at[slot, j], o_slope.at[j, at], act_sems.at[1, slot, j]),
+        )
+
+    def feed(step):
+        source = place.mate(sources - 1 - step)
+        at = pl.ds(pl.multiple_of(source * span, span), span)
+        hidden = middle[at, :] + nn(mixed[at, :], w_out[...]) + vectors[7:8, :]
+        middle[at, :] = hidden
+        center, speed = moments(hidden)
+        normed = (center * speed * vectors[2:3, :] + vectors[4:5, :]).astype(BF)
+        second[at, :] = normed
+        total = hidden + vectors[8:9, :]
+        for j in range(chunks):
+
+            @pl.when(step >= 2)
+            def _():
+                for copy in act_copies(step - 2, j, at):
+                    copy.wait()
+
+            columns = pl.ds(j * width, width)
+            pre = nn(normed, w_up[:, columns]) + vectors[9 + j : 10 + j, :]
+            value, steep = gelu_and_slope(pre)
+            value = value.astype(BF)
+            act[step % 2, j] = value
+            slope[step % 2, j] = steep.astype(BF)
+            for copy in act_copies(step, j, at):
+                copy.start()
+            total = total + nn(value, w_down[columns, :])
+        result[step] = total.astype(BF)
+
+        @pl.when(step < sources - 1)
+        def _():
+            remote(
+                result.at[step],
+                o_result.at[place.tm],
+                row_sends.at[3, sources - 1 - step],
+                row_recvs.at[3, sources - 1 - step],
+                (place.batch, source),
+            ).start()
+
+    pl.loop(0, sources)(feed)
+    own_result = pltpu.make_async_copy(result.at[sources - 1], o_result.at[place.tm], local_sems.at[0])
+    own_result.start()
+    kept = [
+        (w_qkv, o_qkv),
+        (w_out, o_out),
+        (w_up, o_up),
+        (w_down, o_down),
+        (vectors, o_small),
+        (x, o_x),
+        (code, o_code),
+        (first, o_first),
+        (q, o_q),
+        (k, o_k),
+        (v, o_v),
+        (mixed, o_mixed),
+        (second, o_second),
+        (rate, o_rate),
+        (middle, o_middle),
+    ]
+    copies = [pltpu.make_async_copy(src, dst, local_sems.at[4 + i]) for i, (src, dst) in enumerate(kept)]
+    for copy in copies:
+        copy.start()
+    own_result.wait()
+    own_part(2).wait()
+    for p in (pairs - 2, pairs - 1):
+        expon_copy(p).wait()
+    for step in (sources - 2, sources - 1):
+        source = place.mate(sources - 1 - step)
+        at = pl.ds(pl.multiple_of(source * span, span), span)
+        for j in range(chunks):
+            for copy in act_copies(step, j, at):
+                copy.wait()
+    for step in range(1, sources):
+        row_wait(2, step)
+        remote(
+            result.at[0],
+            o_result.at[place.mate(step)],
+            row_sends.at[3, step],
+            row_recvs.at[3, step],
+            place.device(),
+        ).wait_recv()
+        for kind in (0, 1, 2):
+            row_copy(kind, step, place.mate(step)).wait_send()
+        remote(
+            result.at[0], o_result.at[place.tm], row_sends.at[3, step], row_recvs.at[3, step], place.device()
+        ).wait_send()
+    for copy in copies:
+        copy.wait()
+    for gather in gathers:
+        gather.drain()
+
+
+def forward(deep, patches, cotangent, code, small, qkv, out, up, down):
+    sources, span, width = patches.shape
+    rows = sources * span
+    chips = deep * 4
+    inner = up.shape[1]
+    chunks = inner // width
+    shape = jax.ShapeDtypeStruct
+    shards = (qkv, out, up, down)
+    fulls = [(2 * chips * s.shape[0], s.shape[1]) for s in shards]
+    plane = (rows, width)
+    outs = [shape(f, BF) for f in fulls]
+    outs += [shape(small.shape, F32), shape(plane, BF), shape(plane, BF), shape(code.shape, F32)]
+    outs += [shape(plane, BF)] * 6 + [shape(plane, F32)] * 2
+    outs += [shape((chunks, rows, width), BF)] * 2
+    outs += [shape((HEADS, rows, rows), BF), shape(patches.shape, BF)]
+    scratch = [pltpu.VMEM(f, BF) for f in fulls]
+    scratch += [pltpu.VMEM((2 * s.shape[0], s.shape[1] // 2), F32) for s in shards]
+    scratch += [
+        pltpu.VMEM((5,) + small.shape, F32),
+        pltpu.VMEM((2 + deep,) + small.shape, F32),
+        pltpu.VMEM(plane, BF),
+        pltpu.VMEM(code.shape, F32),
+    ]
+    scratch += [pltpu.VMEM(plane, BF)] * 6 + [pltpu.VMEM(plane, F32)] * 2
+    scratch += [
+        pltpu.VMEM((2, 2, rows, rows), BF),
+        pltpu.VMEM((2, chunks, span, width), BF),
+        pltpu.VMEM((2, chunks, span, width), BF),
+        pltpu.VMEM((sources, span, width), BF),
+        pltpu.VMEM((2, rows, 128), BF),
+        pltpu.VMEM((2, rows, 128), BF),
+    ]
+    dma = pltpu.SemaphoreType.DMA
+    scratch += [
+        dma((4,)),
+        dma((4, 1 + 2 * chips)),
+        dma((4, 1 + 2 * chips)),
+        dma((2 + deep,)),
+        dma((2 + deep,)),
+        dma((4, sources)),
+        dma((4, sources)),
+        dma((20,)),
+        dma((2,)),
+        dma((2, 2, chunks)),
+    ]
+    return pl.pallas_call(
+        functools.partial(forward_kernel, deep),
+        out_shape=outs,
+        in_specs=[HBM] * 8,
+        out_specs=[HBM] * len(outs),
+        scratch_shapes=scratch,
+        compiler_params=pltpu.CompilerParams(
+            collective_id=0, has_side_effects=True, vmem_limit_bytes=62 * 2**20
+        ),
+        name="forward",
+    )(patches, cotangent, code, small, qkv, out, up, down)
+
+
+class Scatter:
+    def __init__(self, place, route, held, slots, final, sends, recvs):
+        self.place, self.route = place, route
+        self.held, self.slots, self.final = held, slots, final
+        self.sends, self.recvs = sends, recvs
+        self.rows = slots.shape[1]
+        self.sent = []
+
+    def region(self, shifts):
+        return pl.ds(pl.multiple_of(self.route.chip(shifts) * self.rows, 16), self.rows)
+
+    def parts(self, stage):
+        route = self.route
+        for d in range(1, route.sizes[stage]):
+            for earlier in route.offsets(stage):
+                offset = list(earlier)
+                offset[stage] = d
+                back = [-o for o in earlier]
+                yield d, back, route.index(offset) - 1
+
+    def send(self, stage):
+        for d, back, slot in self.parts(stage):
+            shifts = list(back)
+            shifts[stage] = d
+            to = [0, 0, 0]
+            to[stage] = d
+            copy = remote(
+                self.held.at[self.region(shifts)],
+                self.slots.at[slot],
+                self.sends.at[slot],
+                self.recvs.at[slot],
+                self.route.device(to),
+            )
+            copy.start()
+            self.sent.append(copy)
+
+    def add(self, stage):
+        found = {}
+        for _, back, slot in self.parts(stage):
+            remote(
+                self.slots.at[slot],
+                self.slots.at[slot],
+                self.sends.at[slot],
+                self.recvs.at[slot],
+                self.place.device(),
+            ).wait_recv()
+            found.setdefault(tuple(back), []).append(slot)
+        for back, slots in found.items():
+            at = self.region(back)
+            total = self.held[at, :].astype(F32)
+            for slot in slots:
+                total = total + self.slots[slot].astype(F32)
+            if stage == 0:
+                self.final[...] = total
+            else:
+                self.held[at, :] = total.astype(BF)
+
+    def drain(self):
+        for copy in self.sent:
+            copy.wait_send()
+
+
+def backward_kernel(
+    deep,
+    i_qkv,
+    i_out,
+    i_up,
+    i_down,
+    i_small,
+    i_x,
+    i_cot,
+    i_code,
+    i_first,
+    i_q,
+    i_k,
+    i_v,
+    i_mixed,
+    i_second,
+    i_rate,
+    i_middle,
+    i_act,
+    i_slope,
+    i_expon,
+    o_qkv,
+    o_out,
+    o_up,
+    o_down,
+    o_small,
+    o_patch,
+    w_qkv,
+    w_out,
+    w_up,
+    w_down,
+    upstream,
+    second,
+    gathered,
+    middle,
+    expon,
+    score_grad,
+    trio,
+    rate,
+    mixed,
+    staged,
+    h_qkv,
+    h_out,
+    h_up,
+    h_down,
+    s_qkv,
+    s_out,
+    s_up,
+    s_down,
+    f_qkv,
+    f_out,
+    f_up,
+    f_down,
+    vectors,
+    code,
+    small,
+    small_slots,
+    patch,
+    load_sems,
+    chunk_sems,
+    pair_sems,
+    hand_sends,
+    hand_recvs,
+    scatter_sends,
+    scatter_recvs,
+    final_sends,
+    final_recvs,
+    small_sends,
+    small_recvs,
+    row_sends,
+    row_recvs,
+    local_sems,
+):
+    place = Place(deep)
+    rows, width = upstream.shape
+    sources, span = patch.shape[:2]
+    half = width // HEADS
+    pairs = HEADS // 2
+    chunks = i_act.shape[0]
+    part = width // 2
+    first = second
+    mixed_grad = upstream
+    first_grad = gathered
+
+    loads = [
+        pltpu.make_async_copy(src, dst, load_sems.at[i])
+        for i, (src, dst) in enumerate(
+            (
+                (i_cot, upstream),
+                (i_second, second),
+                (i_middle, middle),
+                (i_small, vectors),
+                (i_code, code),
+                (i_out, w_out),
+                (i_qkv, w_qkv),
+            )
+        )
+    ]
+
+    def chunk_loads(j):
+        slot = j % 2
+        columns = pl.ds(pl.multiple_of(j * width, 128), width)
+        moves = (
+            (i_down.at[columns], w_down.at[slot]),
+            (i_up.at[:, columns], w_up.at[slot]),
+            (i_act.at[j], expon.at[slot, 0, :, pl.ds(0, width)]),
+            (i_slope.at[j], expon.at[slot, 1, :, pl.ds(0, width)]),
+        )
+        return [pltpu.make_async_copy(src, dst, chunk_sems.at[slot, n]) for n, (src, dst) in enumerate(moves)]
+
+    def pair_loads(p):
+        slot = p % 2
+        lanes = pl.ds(pl.multiple_of(p * 2 * half, 128), 2 * half)
+        moves = (
+            (i_expon.at[pl.ds(2 * p, 2)], expon.at[slot]),
+            (i_q.at[:, lanes], trio.at[slot, 0]),
+            (i_k.at[:, lanes], trio.at[slot, 1]),
+            (i_v.at[:, lanes], trio.at[slot, 2]),
+            (i_rate.at[:, lanes], rate.at[slot]),
+            (i_mixed.at[:, lanes], mixed.at[slot]),
+        )
+        return [pltpu.make_async_copy(src, dst, pair_sems.at[slot, n]) for n, (src, dst) in enumerate(moves)]
+
+    for copy in loads[:2] + chunk_loads(0) + loads[2:]:
+        copy.start()
+    place.enter()
+
+    zpq = Route(place, "zpq", True)
+    pzq = Route(place, "pzq", False)
+    scatters = [
+        Scatter(place, route, held, slots, final, scatter_sends.at[i], scatter_recvs.at[i])
+        for i, (route, held, slots, final) in enumerate(
+            (
+                (zpq, h_qkv, s_qkv, f_qkv),
+                (zpq, h_out, s_out, f_out),
+                (zpq, h_up, s_up, f_up),
+                (pzq, h_down, s_down, f_down),
+            )
+        )
+    ]
+    by_qkv, by_out, by_up, by_down = scatters
+
+    def columns(c):
+        return pl.ds(pl.multiple_of(c * part, 128), part)
+
+    def hand(slot, held, n):
+        return remote(
+            staged.at[slot, :, columns(1 - place.c)],
+            held,
+            hand_sends.at[n],
+            hand_recvs.at[n],
+            place.device(c=1 - place.c),
+        )
+
+    def settle(slot, held, n):
+        copy = hand(slot, held, n)
+        copy.wait_recv()
+        held[...] = (held[...].astype(F32) + staged[slot, :, columns(place.c)].astype(F32)).astype(BF)
+        copy.wait_send()
+
+    def down_chunk(j):
+        return (2 * (j % 2), h_down.at[pl.ds(pl.multiple_of(j * width, 128), width)], j)
+
+    def up_chunk(j):
+        return (2 * (j % 2) + 1, h_up.at[:, pl.ds(pl.multiple_of(j * part, 128), part)], chunks + j)
+
+    def qkv_chunk(i):
+        return (1 + i, h_qkv.at[:, pl.ds(pl.multiple_of(i * part, 128), part)], 2 * chunks + 1 + i)
+
+    out_chunk = (0, h_out, 2 * chunks)
+
+    for copy in loads[:2]:
+        copy.wait()
+
+    def feed(j):
+        @pl.when(j < chunks - 1)
+        def _():
+            for copy in chunk_loads(j + 1):
+                copy.start()
+
+        for copy in chunk_loads(j):
+            copy.wait()
+        slot = j % 2
+        act_grad = nt(upstream[...], w_down[slot]).astype(BF).astype(F32)
+        pre_grad = (act_grad * expon[slot, 1, :, 0:width].astype(F32)).astype(BF)
+        small[0, pl.ds(9 + j, 1), :] = column_sum(pre_grad.astype(F32))
+        staged[down_chunk(j)[0]] = tn(expon[slot, 0, :, 0:width], upstream[...]).astype(BF)
+        hand(*down_chunk(j)).start()
+        staged[up_chunk(j)[0]] = tn(second[...], pre_grad).astype(BF)
+        hand(*up_chunk(j)).start()
+        grown = nt(pre_grad, w_up[slot])
+
+        @pl.when(j == 0)
+        def _():
+            gathered[...] = grown
+
+        @pl.when(j > 0)
+        def _():
+            gathered[...] = gathered[...] + grown
+            settle(*down_chunk(j - 1))
+            settle(*up_chunk(j - 1))
+
+    pl.loop(0, chunks)(feed)
+    whole_mixed = pltpu.make_async_copy(i_mixed, expon.at[1, 1, :, pl.ds(0, width)], local_sems.at[0])
+    whole_mixed.start()
+    for copy in pair_loads(0):
+        copy.start()
+    load_first = pltpu.make_async_copy(i_first, first, local_sems.at[1])
+    load_first.start()
+    for copy in loads[2:]:
+        copy.wait()
+    settle(*down_chunk(chunks - 1))
+    settle(*up_chunk(chunks - 1))
+    by_down.send(2)
+    by_up.send(2)
+
+    for row in (0, 1, 2, 3, 4, 5, 6, 7, 8, 13, 14, 15):
+        small[0, row : row + 1, :] = jnp.zeros((1, width), F32)
+
+    def bend(n):
+        at = pl.ds(pl.multiple_of(n * span, span), span)
+        center, speed = moments(middle[at, :])
+        normed = center * speed
+        grad = gathered[at, :]
+        small[0, 2:3, :] = small[0, 2:3, :] + column_sum(grad * normed)
+        small[0, 4:5, :] = small[0, 4:5, :] + column_sum(grad)
+        above = upstream[at, :].astype(F32)
+        small[0, 8:9, :] = small[0, 8:9, :] + column_sum(above)
+        total = above + norm_back(normed, speed, vectors[2:3, :], grad)
+        middle[at, :] = total
+        low_total = total.astype(BF)
+        small[0, 7:8, :] = small[0, 7:8, :] + column_sum(low_total.astype(F32))
+        mixed_grad[at, :] = nt(low_total, w_out[...]).astype(BF)
+
+    pl.loop(0, sources)(bend)
+    whole_mixed.wait()
+    staged[0] = tn(expon[1, 1, :, 0:width], middle[...].astype(BF)).astype(BF)
+    hand(*out_chunk).start()
+    load_first.wait()
+
+    lane = lax.broadcasted_iota(jnp.int32, (1, 2 * half), 1)
+    low = lane < half
+    own_lanes = [low.astype(F32), 1.0 - low.astype(F32)]
+    block = min(rows, 512)
+
+    def attend(p):
+        slot = p % 2
+        lanes = pl.ds(pl.multiple_of(p * 2 * half, 128), 2 * half)
+
+        @pl.when(p < pairs - 1)
+        def _():
+            for copy in pair_loads(p + 1):
+                copy.start()
+
+        for copy in pair_loads(p):
+            copy.wait()
+        scaled = (mixed_grad[:, lanes].astype(F32) * rate[slot]).astype(BF)
+        product = scaled.astype(F32) * mixed[slot].astype(F32)
+        query, key, value = trio[slot, 0], trio[slot, 1], trio[slot, 2]
+        key_grads, value_grads, query_grads = [], [], []
+        for h in range(2):
+            inner = jnp.sum(product * own_lanes[h], -1, keepdims=True)
+            lone = scaled * own_lanes[h].astype(BF)
+            query_parts = []
+            for n in range(rows // block):
+                at = slice(n * block, (n + 1) * block)
+                grad = nt(lone[at], value)
+                weights = expon[slot, h, at, :].astype(F32)
+                grad = (weights * (grad - inner[at])).astype(BF)
+                score_grad[h, at, :] = grad
+                query_parts.append(nn(grad, key))
+            query_grads.append(jnp.concatenate(query_parts, 0))
+            key_grads.append(tn(query, score_grad[h]))
+            value_grads.append(tn(scaled, expon[slot, h]))
+        query_grad = (jnp.where(low, query_grads[0], query_grads[1]) * (1.0 / math.sqrt(half))).astype(BF)
+        key_grad = jnp.concatenate([key_grads[0][:half], key_grads[1][half:]], 0).T.astype(BF)
+        value_grad = jnp.concatenate([value_grads[0][:half], value_grads[1][half:]], 0).T.astype(BF)
+        small[0, 5:6, lanes] = column_sum(query_grad.astype(F32))
+        small[0, 6:7, lanes] = column_sum(value_grad.astype(F32))
+        grads = jnp.concatenate([query_grad, key_grad, value_grad], 1)
+        where = pl.ds(pl.multiple_of(slot * part, 128), part)
+        staged[1 + p // 2, :, where] = tn(first[...], grads).astype(BF)
+        weight = jnp.concatenate(
+            [w_qkv[:, pl.ds(pl.multiple_of(p * 2 * half + n * width, 128), 2 * half)] for n in range(3)], 1
+        )
+        grown = nt(grads, weight)
+
+        @pl.when(p == 0)
+        def _():
+            first_grad[...] = grown
+
+        @pl.when(p > 0)
+        def _():
+            first_grad[...] = first_grad[...] + grown
+
+        @pl.when(p % 2 == 1)
+        def _():
+            hand(*qkv_chunk(p // 2)).start()
+
+    pl.loop(0, pairs)(attend)
+    load_x = pltpu.make_async_copy(i_x, expon.at[0, 0, :, pl.ds(0, width)], local_sems.at[2])
+    load_x.start()
+    load_x.wait()
+    settle(*out_chunk)
+    for i in range(3):
+        settle(*qkv_chunk(i))
+    by_out.send(2)
+    by_qkv.send(2)
+
+    def close(step):
+        source = place.mate(sources - 1 - step)
+        at = pl.ds(pl.multiple_of(source * span, span), span)
+        turned = jnp.transpose(code[source])
+        flags = jnp.concatenate([turned[:, 0:1], turned[:, 1:2]], 0) == 1.0
+        start = jnp.where(flags, vectors[0:1, :], expon[0, 0, at, 0:width].astype(F32))
+        center, speed = moments(start)
+        normed = center * speed
+        grad = first_grad[at, :]
+        small[0, 1:2, :] = small[0, 1:2, :] + column_sum(grad * normed)
+        small[0, 3:4, :] = small[0, 3:4, :] + column_sum(grad)
+        total = middle[at, :] + norm_back(normed, speed, vectors[1:2, :], grad)
+        small[0, 0:1, :] = small[0, 0:1, :] + column_sum(jnp.where(flags, total, 0.0))
+        patch[step] = jnp.where(flags, 0.0, total).astype(BF)
+
+        @pl.when(step < sources - 1)
+        def _():
+            remote(
+                patch.at[step],
+                o_patch.at[place.tm],
+                row_sends.at[sources - 1 - step],
+                row_recvs.at[sources - 1 - step],
+                (place.batch, source),
+            ).start()
+
+    pl.loop(0, sources)(close)
+    own_patch = pltpu.make_async_copy(patch.at[sources - 1], o_patch.at[place.tm], local_sems.at[3])
+    own_patch.start()
+    sum_vectors(place, small, small_slots, small_sends, small_recvs)
+    own_small = pltpu.make_async_copy(small.at[4], o_small, local_sems.at[4])
+    own_small.start()
+    for stage in (2, 1, 0):
+        for scatter in scatters:
+            scatter.add(stage)
+        if stage > 0:
+            for scatter in scatters:
+                scatter.send(stage - 1)
+
+    moves = []
+
+    def deliver(final, target, pieces):
+        shard = target.shape[0]
+        for near, far, jump, size in pieces:
+            to = pl.ds(pl.multiple_of(far + place.c * jump, 128), size)
+            mine = pl.ds(pl.multiple_of(place.c * shard, 8), shard)
+            theirs = pl.ds(pl.multiple_of((1 - place.c) * shard, 8), shard)
+            n = len(moves) // 2
+            moves.append(
+                pltpu.make_async_copy(final.at[mine, pl.ds(near, size)], target.at[:, to], local_sems.at[5 + n])
+            )
+            moves.append(
+                remote(
+                    final.at[theirs, pl.ds(near, size)],
+                    target.at[:, to],
+                    final_sends.at[n],
+                    final_recvs.at[n],
+                    place.device(c=1 - place.c),
+                )
+            )
+            moves[-2].start()
+            moves[-1].start()
+
+    deliver(f_down, o_down, [(0, 0, part, part)])
+    deliver(f_up, o_up, [(j * part, j * width, part, part) for j in range(chunks)])
+    deliver(f_out, o_out, [(0, 0, part, part)])
+    deliver(
+        f_qkv,
+        o_qkv,
+        [
+            (i * part + n * 2 * half, n * width + i * 4 * half, 2 * half, 2 * half)
+            for i in range(3)
+            for n in range(3)
+        ],
+    )
+    for move in moves:
+        move.wait()
+    for step in range(1, sources):
+        copy = remote(
+            patch.at[0], o_patch.at[place.mate(step)], row_sends.at[step], row_recvs.at[step], place.device()
+        )
+        copy.wait_recv()
+        copy.wait_send()
+    own_patch.wait()
+    own_small.wait()
+    for scatter in scatters:
+        scatter.drain()
+
+
+def backward(deep, saved, shards, patches):
+    sources, span, width = patches.shape
+    rows = sources * span
+    chips = deep * 4
+    chunks = shards[2].shape[1] // width
+    shape = jax.ShapeDtypeStruct
+    plane = (rows, width)
+    small = saved[4]
+    code = saved[7]
+    halves = [(2 * chips * s.shape[0], s.shape[1] // 2) for s in shards]
+    outs = [shape(s.shape, F32) for s in shards] + [shape(small.shape, F32), shape(patches.shape, BF)]
+    scratch = [
+        pltpu.VMEM(saved[0].shape, BF),
+        pltpu.VMEM(saved[1].shape, BF),
+        pltpu.VMEM((2, width, width), BF),
+        pltpu.VMEM((2, width, width), BF),
+        pltpu.VMEM(plane, BF),
+        pltpu.VMEM(plane, BF),
+        pltpu.VMEM(plane, F32),
+        pltpu.VMEM(plane, F32),
+        pltpu.VMEM((2, 2, rows, rows), BF),
+        pltpu.VMEM((2, rows, rows), BF),
+        pltpu.VMEM((2, 3, rows, 2 * width // HEADS), BF),
+        pltpu.VMEM((2, rows, 2 * width // HEADS), F32),
+        pltpu.VMEM((2, rows, 2 * width // HEADS), BF),
+        pltpu.VMEM((4, width, width), BF),
+    ]
+    scratch += [pltpu.VMEM(h, BF) for h in halves]
+    scratch += [pltpu.VMEM((chips - 1, 2 * s.shape[0], s.shape[1] // 2), BF) for s in shards]
+    scratch += [pltpu.VMEM((2 * s.shape[0], s.shape[1] // 2), F32) for s in shards]
+    scratch += [
+        pltpu.VMEM(small.shape, F32),
+        pltpu.VMEM(code.shape, F32),
+        pltpu.VMEM((5,) + small.shape, F32),
+        pltpu.VMEM((2 + deep,) + small.shape, F32),
+        pltpu.VMEM(patches.shape, BF),
+    ]
+    dma = pltpu.SemaphoreType.DMA
+    scratch += [
+        dma((7,)),
+        dma((2, 4)),
+        dma((2, 6)),
+        dma((2 * chunks + 4,)),
+        dma((2 * chunks + 4,)),
+        dma((4, chips - 1)),
+        dma((4, chips - 1)),
+        dma((11 + chunks,)),
+        dma((11 + chunks,)),
+        dma((2 + deep,)),
+        dma((2 + deep,)),
+        dma((sources,)),
+        dma((sources,)),
+        dma((16 + chunks,)),
+    ]
+    return pl.pallas_call(
+        functools.partial(backward_kernel, deep),
+        out_shape=outs,
+        in_specs=[HBM] * len(saved),
+        out_specs=[HBM] * len(outs),
+        scratch_shapes=scratch,
+        compiler_params=pltpu.CompilerParams(
+            collective_id=1, has_side_effects=True, vmem_limit_bytes=63 * 2**20
+        ),
+        name="backward",
+    )(*saved)
+
+
+def pack(deep, mask_embed, norm_gain, norm_shift, qv_bias, branch_bias, up_bias, width):
+    device = lax.axis_index("batch") * 4 + lax.axis_index("tm")
+    lines = jnp.concatenate([mask_embed[None], norm_gain, norm_shift, qv_bias, branch_bias], 0)
+    lines = lines.astype(BF).astype(F32)
+    top = lax.dynamic_update_slice(jnp.zeros((9, width), F32), lines, (0, device * lines.shape[1]))
+    flat = lax.dynamic_update_slice(
+        jnp.zeros((7 * width,), F32), up_bias.astype(BF).astype(F32), (device * up_bias.shape[0],)
+    )
+    return jnp.concatenate([top, flat.reshape(7, width)], 0)
+
+
+def by_rows(
+    deep,
+    patches,
+    segment_ids,
+    mask_flags,
+    cotangent,
+    mask_embed,
+    norm_gain,
+    norm_shift,
+    qkv_weight,
+    qv_bias,
+    out_weight,
+    branch_bias,
+    up_weight,
+    up_bias,
+    down_weight,
+):
+    sources, span, width = patches.shape
+    shards = (qkv_weight, out_weight, up_weight, down_weight)
+    lane = 128
+    code = jnp.concatenate([mask_flags.reshape(sources, -1, lane), segment_ids.reshape(sources, -1, lane)], 1)
+    code = jnp.pad(code.astype(F32), ((0, 0), (0, 8 - code.shape[1]), (0, 0)))
+    small = pack(deep, mask_embed, norm_gain, norm_shift, qv_bias, branch_bias, up_bias, width)
+    *saved, result = forward(deep, patches, cotangent, code, small, *shards)
+    *grads, sums, patch_grad = backward(deep, saved, shards, patches)
+    device = lax.axis_index("batch") * 4 + lax.axis_index("tm")
+    piece = mask_embed.shape[0]
+    own = lax.dynamic_slice(sums, (0, device * piece), (9, piece))
+    up_sum = lax.dynamic_slice(sums[9:].reshape(-1), (device * up_bias.shape[0],), up_bias.shape)
+    return (
+        result.astype(F32),
+        patch_grad.astype(F32),
+        own[0],
+        own[1:3],
+        own[3:5],
+        grads[0],
+        own[5:7],
+        grads[1],
+        own[7:9],
+        grads[2],
+        up_sum,
+        grads[3],
+    )
 
 
 def layer_norm(hidden, gain, shift):
@@ -34,7 +1239,7 @@
     )
 
 
-def on_device(
+def by_patches(
     patches,
     segment_ids,
     mask_flags,
@@ -113,7 +1318,7 @@
             * scale
         )
         allowed = (query_seg[:, :, None] == key_seg[:, None, :])[:, None]
-        return jnp.where(allowed, scores, NEGATIVE)
+        return jnp.where(allowed, scores, FAR)
 
     def attend(items):
         query_blk, pair_blk, own_seg, far_seg = items
@@ -279,6 +1484,13 @@
 
 
 def solution(mesh):
+    wide, deep = mesh.shape["batch"] * mesh.shape["tm"], mesh.shape["batch"] // 2
+
+    def on_device(patches, *rest):
+        width = patches.shape[-1]
+        fits = mesh.shape["tm"] == patches.shape[0] == 4 and width % (8 * wide) == 0 and patches.shape[1] == 256
+        return by_rows(deep, patches, *rest) if fits else by_patches(patches, *rest)
+
     return jax.shard_map(
         on_device,
         mesh=mesh,

time: 1450 us -> 333 us (0.23)
  waiting for transfers between devices: 670 us -> 0 us
  Pallas kernels: 0 us -> 314 us
  matrix products: 285 us -> 0 us
  blocking collectives: 232 us -> 0 us
  other arithmetic: 121 us -> 10.2 us
  local copies, waits for them, and re-layouts: 117 us -> 7.08 us
    reduce_scatter x5 -> x0, waiting for transfers between devices: 584 us -> none  [the longest x1 146 us: on_device(): lax.psum_scatter(pair_grads, 'tm', scatter_dimension=1, tiled=True)]
    pallas_call x0 -> x2, Pallas kernels: none -> 314 us  [the longest x1 166 us: backward(): pl.pallas_call(functools.partial(backward_kernel, deep), out_shape=outs,...]
    dot_general x26 -> x0, matrix products: 285 us -> none  [the longest x4 41.5 us: masked_scores(): jnp.einsum('bqhd,bkhd->bhqk', query_heads, key_heads, preferred_element_t...]
    all_gather x5 -> x0, blocking collectives: 151 us -> none  [the longest x1 39.7 us: on_device(): lax.all_gather(norm_shift.astype(jnp.bfloat16), ('batch', 'tm'), axis=1,...]
    all_gather x5 -> x0, waiting for transfers between devices: 85.4 us -> none  [the longest x1 35.9 us: on_device(): lax.all_gather(pairs, 'tm', axis=1, tiled=True)]
    unnamed x2 -> x0, blocking collectives: 80.8 us -> none
    dynamic_update_slice x12 -> x1, local copies, waits for them, and re-layouts: 53.3 us -> 0.33 us  [pack(): lax.dynamic_update_slice(jnp.zeros((9, width), F32), lines, (0, device *...]
    convert_element_type x14 -> x4, other arithmetic: 46 us -> 5.4 us  [the longest x1 3.46 us: by_rows(): patch_grad.astype(F32)]
  transfers between devices with their start and end apart: 10 -> 0, of which waited for: 8 -> 0; matrix products, arithmetic and copies ran while one was open for 15% -> 0% of each run, Pallas kernels for 0% -> 0%
where the time goes in v1:
time: 333 us; the launch traced here: 332 us
  Pallas kernels  314 us (94%)
  other arithmetic  10.2 us (3%)
  local copies, waits for them, and re-layouts  7.08 us (2%)
    pallas_call x1, Pallas kernels, backward(): pl.pallas_call(functools.partial(backward_kernel, deep), out_shape=outs,...  166 us
    pallas_call x1, Pallas kernels, forward(): pl.pallas_call(functools.partial(forward_kernel, deep), out_shape=outs, i...  148 us

profile of v1, /device:TPU:11, one launch (start us, length us, event | category | flops | bytes accessed | tf_op | source)
XLA Modules:
  0.0 332.1 jit_solution(13051430614518179547)
XLA Ops:
  0.7 0.7 convert.17
  1.3 0.7 convert.18
  2.0 0.7 convert.19
  2.7 0.7 convert.20
  3.4 0.7 convert_bitcast_fusion
  4.0 0.1 concatenate.11
  4.2 0.3 dynamic_update_slice.6
  4.5 0.8 convert_dynamic-update-slice_fusion
  5.3 0.6 pad_maximum_fusion.small_in
  5.9 0.7 reshape.36
  6.6 0.7 reshape.37
  7.4 0.6 pad.4.code_in
  8.0 147.6 %forward.1 = (bf16[768,2304]{1,0:T(8,128)(2,1)}, bf16[768,768]{1,0:T(8,128)(2,1)}, bf16[768,3072]{1,0:T(8,128)(2,1)}, bf16[3072,768]{1,0:T(8,128)(2,1)}, f32[16,...) custom-call(bf16[4,256,768]{2,1,0:T(8,128)(2,1)} %patches.1, ...), custom_call_target="tpu_custom_call" | custom-call | tf_op jit(solution)/shard_map/forward/pallas_call | solution.py:625
  155.6 166.5 %backward.1 = (f32[24,2304]{1,0:T(8,128)}, f32[24,768]{1,0:T(8,128)}, f32[24,3072]{1,0:T(8,128)}, f32[96,768]{1,0:T(8,128)}, f32[16,768]{1,0:T(8,128)}, /*index=5*/bf16[4,256,768]{2,1,0:T(8,128)(2,1)}) custom-call(bf16[768,2304]{1,0:T(8,128)(2,1)} %get-tuple-element.39.i_qkv, bf16[768,768]{1,0:T(8,128)(2,1)} %get-tuple-element.40.i_out, ...), custom_call_target="tpu_custom_call" | custom-call | tf_op jit(solution)/shard_map/backward/pallas_call | solution.py:1151
  322.1 3.5 %convert_element_type.26 = f32[4,256,768]{2,1,0:T(8,128)} convert(bf16[4,256,768]{2,1,0:T(8,128)(2,1)} %get-tuple-element.58) | non-fusion elementwise | flops 786432 | bytes 4718592 | tf_op jit(solution)/shard_map/convert_element_type | solution.py:1206
  325.6 0.6 dynamic_slice.7
  326.2 0.7 fusion
  326.8 0.6 dynamic-slice_bitcast_fusion
  327.4 0.0 copy-done
  327.4 1.9 convert_element_type.25
  329.4 0.7 copy.32
  330.0 0.6 copy.33
  330.7 0.7 copy.34
  331.4 0.7 copy.35
  (18 shorter events, 0.1 us)
Async XLA Ops:
  322.1 3.5 %copy-start.5 = (f32[16,768]{1,0:T(8,128)S(1)}, f32[16,768]{1,0:T(8,128)}, u32[]{:S(2)}) copy-start(f32[16,768]{1,0:T(8,128)} %get-tuple-element.59) | copy-start | bytes 147460
  322.1 5.3 %copy-start = (bf16[4,256,768]{2,1,0:T(8,128)(2,1)S(1)}, bf16[4,256,768]{2,1,0:T(8,128)(2,1)}, u32[]{:S(2)}) copy-start(bf16[4,256,768]{2,1,0:T(8,128)(2,1)} %get-tuple-element.38) | copy-start | bytes 4718596
  327.4 2.0 copy-start.3
  327.4 2.6 copy-start.4
  327.4 3.3 copy-start.2
  327.4 4.0 %copy-start.1 = (f32[96,768]{1,0:T(8,128)S(1)}, f32[96,768]{1,0:T(8,128)}, u32[]{:S(2)}) copy-start(f32[96,768]{1,0:T(8,128)} %get-tuple-element.91) | copy-start | bytes 884740

commit v2 on v1

--- a/solution.py
+++ b/solution.py
@@ -28,6 +28,174 @@
 )
 
 
+FORWARD_STEPS = {
+    "start": {
+        0: [
+            ("first", "vector"),
+            ("first", "qkv"),
+            ("first", "out"),
+            ("first", "up"),
+            (0, "vector", 0, 3),
+            (0, "qkv", 0, 3),
+            (0, "out", 0, 3),
+            (1, "vector", 0, 4),
+            (1, "qkv", 0, 2),
+            (1, "qkv", 2, 4),
+            ("rows",),
+            ("first", "down"),
+            (2, "vector", 0, 8),
+            (1, "out", 0, 2),
+            (1, "out", 2, 4),
+            ("finish", "vector"),
+            (2, "qkv", 0, 4),
+            ("spread",),
+            (2, "qkv", 4, 8),
+            ("finish", "qkv"),
+        ],
+    },
+    "project": {
+        2: [
+            (0, "up", 0, 3),
+        ],
+    },
+    "attend": {
+        0: [
+            (0, "down", 0, 1),
+        ],
+        2: [
+            (2, "out", 0, 4),
+            (2, "out", 4, 8),
+        ],
+        3: [
+            ("finish", "out"),
+            (1, "up", 0, 2),
+        ],
+        5: [
+            (1, "up", 2, 4),
+            (1, "down", 0, 3),
+        ],
+        8: [
+            (1, "down", 3, 6),
+            (2, "up", 0, 4),
+        ],
+        9: [
+            (2, "up", 4, 8),
+        ],
+        10: [
+            ("finish", "up"),
+            ("cotangent",),
+        ],
+    },
+    "rise": {
+        1: [
+            (2, "down", 0, 4),
+        ],
+        2: [
+            (2, "down", 4, 8),
+        ],
+        3: [
+            ("finish", "down"),
+        ],
+    },
+}
+
+
+BACKWARD_STEPS = {
+    "feed": {
+        2: [
+            ("settle", "up", 0),
+        ],
+        5: [
+            ("settle", "down", 0),
+        ],
+        6: [
+            ("settle", "down", 1),
+        ],
+        7: [
+            ("turn", 0),
+            ("settle", "up", 1),
+            ("settle", "down", 2),
+        ],
+        9: [
+            ("turn", 1),
+            ("add", "up", 2, 0),
+        ],
+        11: [
+            ("turn", 2),
+            ("settle", "down", 3),
+            ("settle", "up", 2),
+        ],
+    },
+    "attend": {
+        1: [
+            ("turn", 3),
+            ("settle", "up", 3),
+        ],
+        4: [
+            ("settle", "out", 0),
+        ],
+        6: [
+            ("add", "up", 2, 3),
+            ("add", "up", 2, 1),
+            ("add", "up", 1, 0),
+            ("settle", "qkv", 0),
+        ],
+        8: [
+            ("add", "up", 1, 1),
+            ("add", "out", 2, 0),
+            ("add", "qkv", 2, 0),
+            ("add", "up", 1, 3),
+        ],
+        9: [
+            ("add", "up", 2, 2),
+        ],
+        10: [
+            ("add", "out", 1, 0),
+            ("add", "down", 1, 0),
+        ],
+    },
+    "close": {
+        0: [
+            ("settle", "qkv", 2),
+        ],
+        1: [
+            ("add", "down", 0, 0),
+        ],
+    },
+    "tail": {
+        0: [
+            ("add", "up", 1, 2),
+            ("add", "up", 0, 0),
+            ("add", "up", 0, 1),
+            ("add", "qkv", 2, 2),
+            ("vector send", 0),
+            ("add", "out", 0, 0),
+            ("settle", "qkv", 1),
+            ("vector add", 0),
+            ("deliver", "out"),
+            ("add", "qkv", 2, 1),
+            ("vector send", 1),
+            ("add", "qkv", 1, 0),
+            ("add", "up", 0, 2),
+            ("deliver", "down"),
+            ("add", "qkv", 1, 2),
+            ("add", "up", 0, 3),
+            ("deliver", "up"),
+            ("vector add", 1),
+            ("add", "qkv", 0, 0),
+            ("vector send", 2),
+            ("vector add", 2),
+            ("vector send", 3),
+            ("add", "qkv", 1, 1),
+            ("add", "qkv", 0, 2),
+            ("add", "qkv", 0, 1),
+            ("deliver", "qkv"),
+            ("vector add", 3),
+        ],
+    },
+}
+
+
 def nn(left, right):
     return jnp.dot(left, right, preferred_element_type=F32)
 
@@ -148,7 +316,6 @@
         self.local, self.sends, self.recvs = local, sends, recvs
         self.rows = shard.shape[0]
         self.half = shard.shape[1] // 2
-        self.sent = []
         self.count = 0
 
     def columns(self, c):
@@ -159,10 +326,8 @@
         return self.full.at[pl.ds(pl.multiple_of(chip * rows, 16), rows), self.columns(c)]
 
     def ship(self, src, dst, recv, device):
-        copy = remote(src, dst, self.sends.at[self.count], recv, device)
-        copy.start()
+        remote(src, dst, self.sends.at[self.count], recv, device).start()
         self.count += 1
-        self.sent.append(copy)
 
     def join(self):
         place = self.place
@@ -202,19 +367,16 @@
         place = self.place
         self.mine.wait()
         own = pl.ds(pl.multiple_of((1 - place.c) * self.rows, 8), self.rows)
-        self.sent[0].wait_send()
         remote(
             self.joined.at[own], self.joined.at[own], self.sends.at[0], self.recvs.at[0], place.device(c=1 - place.c)
-        ).wait_recv()
+        ).wait()
         chip = self.route.chip([0, 0, 0])
         self.region(chip, place.c)[...] = self.joined[...].astype(BF)
         self.arrive((0, 0, 0), -1)
 
-    def stage(self, stage):
+    def stage(self, stage, some=slice(None)):
         route = self.route
-        for offset in route.offsets(stage + 1):
-            if offset[stage] == 0:
-                continue
+        for offset in [o for o in route.offsets(stage + 1) if o[stage] > 0][some]:
             block = self.region(route.chip([-o for o in offset]), self.place.c)
             remote(
                 block, block, self.sends.at[0], self.recvs.at[1 + route.index(offset)], self.place.device()
@@ -235,30 +397,66 @@
             ).wait_recv()
 
     def drain(self):
-        for copy in self.sent[1:]:
-            copy.wait_send()
-
-
-def sum_vectors(place, held, slots, sends, recvs):
-    stages = [
-        [place.device(c=1 - place.c)],
-        [place.device(x=1 - place.x)],
-        [place.device(y=1 - place.y)],
-        [place.device(z=(place.z + d) % place.deep) for d in range(1, place.deep)],
-    ]
-    slot = 0
-    for stage, others in enumerate(stages):
-        copies = []
-        for other in others:
-            copies.append(remote(held.at[stage], slots.at[slot], sends.at[slot], recvs.at[slot], other))
-            copies[-1].start()
-            slot += 1
-        total = held[stage]
-        for copy in copies:
+        block = self.region(self.route.chip([0, 0, 0]), self.place.c)
+        for n in range(1, self.count):
+            remote(block, block, self.sends.at[n], self.recvs.at[0], self.place.device()).wait_send()
+
+
+class VectorSum:
+    def __init__(self, place, held, slots, sends, recvs):
+        self.held, self.slots = held, slots
+        stages = [
+            [place.device(c=1 - place.c)],
+            [place.device(x=1 - place.x)],
+            [place.device(y=1 - place.y)],
+            [place.device(z=(place.z + d) % place.deep) for d in range(1, place.deep)],
+        ]
+        self.copies, slot = [], 0
+        for stage, others in enumerate(stages):
+            self.copies.append([])
+            for other in others:
+                copy = remote(held.at[stage], slots.at[slot], sends.at[slot], recvs.at[slot], other)
+                self.copies[-1].append((copy, slot))
+                slot += 1
+
+    def send(self, stage):
+        for copy, _ in self.copies[stage]:
+            copy.start()
+
+    def add(self, stage):
+        total = self.held[stage]
+        for copy, slot in self.copies[stage]:
             copy.wait()
-        for back in range(len(others)):
-            total = total + slots[slot - len(others) + back]
-        held[stage + 1] = total
+            total = total + self.slots[slot]
+        self.held[stage + 1] = total
+
+
+def gather_vectors(mask_embed, norm_gain, norm_shift, qv_bias, branch_bias, up_bias):
+    lines = jnp.concatenate([mask_embed[None], norm_gain, norm_shift, qv_bias, branch_bias], 0)
+    lines = jnp.pad(lines, ((0, 0), (0, 128 - lines.shape[1])))
+    rest = jnp.concatenate([lines[8:], jnp.pad(up_bias, (0, 128 - up_bias.shape[0]))[None]], 0)
+    return jnp.concatenate([lines[:8], jnp.pad(rest, ((0, 6), (0, 0)))], 1)
+
+
+def spread_vectors(blocks, vectors):
+    width = vectors.shape[1]
+    devices = blocks.shape[0] // 8
+    piece = width // devices
+    table = blocks[...].astype(F32)
+    vectors[...] = jnp.zeros_like(vectors)
+
+    def put(rows, at, start):
+        window = min(start // 128 * 128, width - 256)
+        wide = jnp.concatenate([rows, jnp.zeros_like(rows)], 1)
+        wide = pltpu.roll(wide, start - window, 1)
+        vectors[at, window : window + 256] = vectors[at, window : window + 256] + wide
+
+    for d in range(devices):
+        block = table[8 * d : 8 * d + 8]
+        put(block[:, :128], slice(0, 8), piece * d)
+        put(block[0:1, 128:], slice(8, 9), piece * d)
+        up = 4 * piece * d
+        put(block[1:2, 128:], slice(9 + up // width, 10 + up // width), up % width)
 
 
 def code_columns(code, source):
@@ -273,7 +471,7 @@
     patches,
     cotangent,
     code_in,
-    small_in,
+    shard_vector,
     shard_qkv,
     shard_out,
     shard_up,
@@ -306,8 +504,9 @@
     j_out,
     j_up,
     j_down,
+    j_vector,
+    w_vector,
     small,
-    small_slots,
     x,
     code,
     first,
@@ -319,7 +518,6 @@
     rate,
     middle,
     expon,
-    act,
     slope,
     result,
     q_code,
@@ -327,8 +525,6 @@
     join_sems,
     gather_sends,
     gather_recvs,
-    small_sends,
-    small_recvs,
     row_sends,
     row_recvs,
     local_sems,
@@ -344,8 +540,6 @@
     inner = w_up.shape[1]
     chunks = inner // width
 
-    near = pltpu.make_async_copy(small_in, small.at[0], local_sems.at[0])
-    near.start()
     place.enter()
 
     kinds = ((patches, x), (code_in, code), (cotangent, o_cot))
@@ -371,13 +565,15 @@
         ).wait_recv()
 
     zpq = Route(place, "zpq", True)
-    pzq = Route(place, "pzq", False)
+    zxy = Route(place, "zpq", False)
+    pzq = Route(place, "pzq", True)
     gathers = [
         Gather(place, route, shard, joined, full, join_sems.at[i], gather_sends.at[i], gather_recvs.at[i])
         for i, (route, shard, joined, full) in enumerate(
             (
-                (zpq, shard_qkv, j_qkv, w_qkv),
-                (zpq, shard_out, j_out, w_out),
+                (zpq, shard_vector, j_vector, w_vector),
+                (zxy, shard_qkv, j_qkv, w_qkv),
+                (zxy, shard_out, j_out, w_out),
                 (zpq, shard_up, j_up, w_up),
                 (pzq, shard_down, j_down, w_down),
             )
@@ -385,24 +581,47 @@
     ]
     for gather in gathers:
         gather.join()
-    gathers[0].first()
+    named = dict(zip(("vector", "qkv", "out", "up", "down"), gathers))
+
+    def send_rows(kinds):
+        for kind in kinds:
+            for step in range(1, sources):
+                row_copy(kind, step, place.mate(step)).start()
+
+    def run(steps):
+        for what, *which in steps:
+            if what == "rows":
+                send_rows((1, 0))
+            elif what == "cotangent":
+                send_rows((2,))
+            elif what == "spread":
+                spread_vectors(w_vector, small)
+            elif what == "first":
+                named[which[0]].first()
+            elif what == "finish":
+                named[which[0]].finish()
+            else:
+                named[which[0]].stage(what, slice(which[1], which[2]))
+
+    def after(loop, index, part=0, parts=1):
+        for when, steps in FORWARD_STEPS.get(loop, {}).items():
+            if when % parts == part:
+                pl.when(index == when // parts)(functools.partial(run, steps))
+
     for kind in (1, 0):
         own_part(kind).start()
-        for step in range(1, sources):
-            row_copy(kind, step, place.mate(step)).start()
-    near.wait()
-    sum_vectors(place, small, small_slots, small_sends, small_recvs)
-    gathers[0].stage(0)
-    gathers[0].stage(1)
-    for gather in gathers[1:]:
-        gather.first()
-    own_part(2).start()
-    for step in range(1, sources):
-        row_copy(2, step, place.mate(step)).start()
-    gathers[0].stage(2)
-    gathers[0].finish()
-
-    vectors = small.at[4]
+    run(FORWARD_STEPS["start"][0])
+    keeping = []
+
+    def keep(src, dst):
+        copy = pltpu.make_async_copy(src, dst, local_sems.at[4 + len(keeping)])
+        copy.start()
+        keeping.append(copy)
+
+    keep(w_qkv, o_qkv)
+    keep(small, o_small)
+
+    vectors = small
     lane = lax.broadcasted_iota(jnp.int32, (1, 2 * half), 1)
     low = lane < half
     own_lanes = [low.astype(F32), 1.0 - low.astype(F32)]
@@ -432,12 +651,14 @@
         for h in range(2):
             base = float(half * (1 - h))
             same = clip_lane - base == clips
-            named = jnp.logical_and(clip_lane >= base, clip_lane < base + 5.0)
+            coded = jnp.logical_and(clip_lane >= base, clip_lane < base + 5.0)
             q_code[h, at, :] = jnp.where(same, 1.0, 0.0).astype(BF)
-            k_code[h, at, :] = jnp.where(jnp.logical_and(named, jnp.logical_not(same)), FAR, 0.0).astype(BF)
-
-    for gather in gathers[1:]:
-        gather.stage(0)
+            k_code[h, at, :] = jnp.where(jnp.logical_and(coded, jnp.logical_not(same)), FAR, 0.0).astype(BF)
+        after("project", step)
+
+    for src, dst in ((x, o_x), (code, o_code), (first, o_first), (q, o_q), (k, o_k), (v, o_v)):
+        keep(src, dst)
+
     block = min(rows, 512)
 
     def expon_copy(p):
@@ -471,113 +692,81 @@
             speed = 1.0 / totals
             rate[at, lanes] = speed
             mixed[at, lanes] = (top * speed).astype(BF)
-        expon_copy(p).start()
+            if part == rows // block - 1:
+                expon_copy(p).start()
+            after("attend", p, part, rows // block)
 
     pl.loop(0, pairs)(attend)
-    for stage in (1, 2):
-        for gather in gathers[1:]:
-            gather.stage(stage)
-    for gather in gathers[1:]:
-        gather.finish()
-
-    def act_copies(step, j, at):
-        slot = step % 2
-        return (
-            pltpu.make_async_copy(act.at[slot, j], o_act.at[j, at], act_sems.at[0, slot, j]),
-            pltpu.make_async_copy(slope.at[slot, j], o_slope.at[j, at], act_sems.at[1, slot, j]),
-        )
-
-    def feed(step):
-        source = place.mate(sources - 1 - step)
-        at = pl.ds(pl.multiple_of(source * span, span), span)
+    for src, dst in ((w_out, o_out), (w_up, o_up), (mixed, o_mixed), (rate, o_rate)):
+        keep(src, dst)
+    for p in (pairs - 2, pairs - 1):
+        expon_copy(p).wait()
+
+    def act(j, at):
+        return expon.at[j // 2, j % 2, at, pl.ds(0, width)]
+
+    def slope_copies(step):
+        at = pl.ds(pl.multiple_of(step * span, span), span)
+        return [
+            pltpu.make_async_copy(slope.at[step % 2, j], o_slope.at[j, at], act_sems.at[step % 2, j])
+            for j in range(chunks)
+        ]
+
+    def act_copies(step):
+        at = pl.ds(pl.multiple_of(step * span, span), span)
+        return [pltpu.make_async_copy(act(j, at), o_act.at[j, at], act_sems.at[2, j]) for j in range(chunks)]
+
+    def rise(step):
+        @pl.when(step >= 2)
+        def _():
+            for copy in slope_copies(step - 2):
+                copy.wait()
+
+        at = pl.ds(pl.multiple_of(step * span, span), span)
         hidden = middle[at, :] + nn(mixed[at, :], w_out[...]) + vectors[7:8, :]
         middle[at, :] = hidden
         center, speed = moments(hidden)
         normed = (center * speed * vectors[2:3, :] + vectors[4:5, :]).astype(BF)
         second[at, :] = normed
-        total = hidden + vectors[8:9, :]
         for j in range(chunks):
-
-            @pl.when(step >= 2)
-            def _():
-                for copy in act_copies(step - 2, j, at):
-                    copy.wait()
-
-            columns = pl.ds(j * width, width)
-            pre = nn(normed, w_up[:, columns]) + vectors[9 + j : 10 + j, :]
+            pre = nn(normed, w_up[:, j * width : (j + 1) * width]) + vectors[9 + j : 10 + j, :]
             value, steep = gelu_and_slope(pre)
-            value = value.astype(BF)
-            act[step % 2, j] = value
+            expon[j // 2, j % 2, at, 0:width] = value.astype(BF)
             slope[step % 2, j] = steep.astype(BF)
-            for copy in act_copies(step, j, at):
-                copy.start()
-            total = total + nn(value, w_down[columns, :])
-        result[step] = total.astype(BF)
-
-        @pl.when(step < sources - 1)
-        def _():
-            remote(
-                result.at[step],
-                o_result.at[place.tm],
-                row_sends.at[3, sources - 1 - step],
-                row_recvs.at[3, sources - 1 - step],
-                (place.batch, source),
-            ).start()
-
-    pl.loop(0, sources)(feed)
-    own_result = pltpu.make_async_copy(result.at[sources - 1], o_result.at[place.tm], local_sems.at[0])
-    own_result.start()
-    kept = [
-        (w_qkv, o_qkv),
-        (w_out, o_out),
-        (w_up, o_up),
-        (w_down, o_down),
-        (vectors, o_small),
-        (x, o_x),
-        (code, o_code),
-        (first, o_first),
-        (q, o_q),
-        (k, o_k),
-        (v, o_v),
-        (mixed, o_mixed),
-        (second, o_second),
-        (rate, o_rate),
-        (middle, o_middle),
-    ]
-    copies = [pltpu.make_async_copy(src, dst, local_sems.at[4 + i]) for i, (src, dst) in enumerate(kept)]
-    for copy in copies:
-        copy.start()
-    own_result.wait()
-    own_part(2).wait()
-    for p in (pairs - 2, pairs - 1):
-        expon_copy(p).wait()
+        for copy in slope_copies(step) + act_copies(step):
+            copy.start()
+        after("rise", step)
+
+    def fall(step):
+        at = pl.ds(pl.multiple_of(step * span, span), span)
+        total = middle[at, :] + vectors[8:9, :]
+        for j in range(chunks):
+            total = total + nn(expon[j // 2, j % 2, at, 0:width], w_down[j * width : (j + 1) * width, :])
+        result[at, :] = total.astype(BF)
+
+    pl.loop(0, sources)(rise)
+    keep(second, o_second)
+    keep(middle, o_middle)
+    keep(w_down, o_down)
+    pl.loop(0, sources)(fall)
+    keep(result, o_result)
+    for step in range(sources):
+        for copy in act_copies(step):
+            copy.wait()
     for step in (sources - 2, sources - 1):
-        source = place.mate(sources - 1 - step)
-        at = pl.ds(pl.multiple_of(source * span, span), span)
-        for j in range(chunks):
-            for copy in act_copies(step, j, at):
-                copy.wait()
+        for copy in slope_copies(step):
+            copy.wait()
     for step in range(1, sources):
         row_wait(2, step)
-        remote(
-            result.at[0],
-            o_result.at[place.mate(step)],
-            row_sends.at[3, step],
-            row_recvs.at[3, step],
-            place.device(),
-        ).wait_recv()
         for kind in (0, 1, 2):
             row_copy(kind, step, place.mate(step)).wait_send()
-        remote(
-            result.at[0], o_result.at[place.tm], row_sends.at[3, step], row_recvs.at[3, step], place.device()
-        ).wait_send()
-    for copy in copies:
+    for copy in keeping:
         copy.wait()
     for gather in gathers:
         gather.drain()
 
 
-def forward(deep, patches, cotangent, code, small, qkv, out, up, down):
+def forward(deep, patches, cotangent, code, vector, qkv, out, up, down):
     sources, span, width = patches.shape
     rows = sources * span
     chips = deep * 4
@@ -588,15 +777,16 @@
     fulls = [(2 * chips * s.shape[0], s.shape[1]) for s in shards]
     plane = (rows, width)
     outs = [shape(f, BF) for f in fulls]
-    outs += [shape(small.shape, F32), shape(plane, BF), shape(plane, BF), shape(code.shape, F32)]
+    outs += [shape((16, width), F32), shape(plane, BF), shape(plane, BF), shape(code.shape, F32)]
     outs += [shape(plane, BF)] * 6 + [shape(plane, F32)] * 2
     outs += [shape((chunks, rows, width), BF)] * 2
-    outs += [shape((HEADS, rows, rows), BF), shape(patches.shape, BF)]
+    outs += [shape((HEADS, rows, rows), BF), shape(plane, BF)]
     scratch = [pltpu.VMEM(f, BF) for f in fulls]
     scratch += [pltpu.VMEM((2 * s.shape[0], s.shape[1] // 2), F32) for s in shards]
     scratch += [
-        pltpu.VMEM((5,) + small.shape, F32),
-        pltpu.VMEM((2 + deep,) + small.shape, F32),
+        pltpu.VMEM((16, vector.shape[1] // 2), F32),
+        pltpu.VMEM((16 * chips, vector.shape[1]), BF),
+        pltpu.VMEM((16, width), F32),
         pltpu.VMEM(plane, BF),
         pltpu.VMEM(code.shape, F32),
     ]
@@ -604,23 +794,20 @@
     scratch += [
         pltpu.VMEM((2, 2, rows, rows), BF),
         pltpu.VMEM((2, chunks, span, width), BF),
-        pltpu.VMEM((2, chunks, span, width), BF),
-        pltpu.VMEM((sources, span, width), BF),
+        pltpu.VMEM(plane, BF),
         pltpu.VMEM((2, rows, 128), BF),
         pltpu.VMEM((2, rows, 128), BF),
     ]
     dma = pltpu.SemaphoreType.DMA
     scratch += [
-        dma((4,)),
-        dma((4, 1 + 2 * chips)),
-        dma((4, 1 + 2 * chips)),
-        dma((2 + deep,)),
-        dma((2 + deep,)),
+        dma((5,)),
+        dma((5, 1 + 2 * chips)),
+        dma((5, 1 + 2 * chips)),
         dma((4, sources)),
         dma((4, sources)),
         dma((20,)),
         dma((2,)),
-        dma((2, 2, chunks)),
+        dma((3, chunks)),
     ]
     return pl.pallas_call(
         functools.partial(forward_kernel, deep),
@@ -632,19 +819,25 @@
             collective_id=0, has_side_effects=True, vmem_limit_bytes=62 * 2**20
         ),
         name="forward",
-    )(patches, cotangent, code, small, qkv, out, up, down)
+    )(patches, cotangent, code, vector, qkv, out, up, down)
 
 
 class Scatter:
-    def __init__(self, place, route, held, slots, final, sends, recvs):
+    def __init__(self, place, route, held, slots, final, sends, recvs, piece=None):
         self.place, self.route = place, route
         self.held, self.slots, self.final = held, slots, final
         self.sends, self.recvs = sends, recvs
         self.rows = slots.shape[1]
+        self.width = piece
         self.sent = []
 
     def region(self, shifts):
         return pl.ds(pl.multiple_of(self.route.chip(shifts) * self.rows, 16), self.rows)
+
+    def columns(self, piece):
+        if piece is None:
+            return pl.ds(0, self.held.shape[1])
+        return pl.ds(pl.multiple_of(piece * self.width, 128), self.width)
 
     def parts(self, stage):
         route = self.route
@@ -652,49 +845,88 @@
             for earlier in route.offsets(stage):
                 offset = list(earlier)
                 offset[stage] = d
-                back = [-o for o in earlier]
-                yield d, back, route.index(offset) - 1
-
-    def send(self, stage):
+                yield d, [-o for o in earlier], route.index(offset) - 1
+
+    def copy(self, stage, d, back, slot, piece):
+        shifts, to = list(back), [0, 0, 0]
+        shifts[stage] = to[stage] = d
+        columns = self.columns(piece)
+        n = 0 if piece is None else piece
+        return remote(
+            self.held.at[self.region(shifts), columns],
+            self.slots.at[slot, :, columns],
+            self.sends.at[n, slot],
+            self.recvs.at[n, slot],
+            self.route.device(to),
+        )
+
+    def send(self, stage, piece=None):
+        self.sent.append((stage, piece))
         for d, back, slot in self.parts(stage):
-            shifts = list(back)
-            shifts[stage] = d
-            to = [0, 0, 0]
-            to[stage] = d
-            copy = remote(
-                self.held.at[self.region(shifts)],
-                self.slots.at[slot],
-                self.sends.at[slot],
-                self.recvs.at[slot],
-                self.route.device(to),
-            )
-            copy.start()
-            self.sent.append(copy)
-
-    def add(self, stage):
+            self.copy(stage, d, back, slot, piece).start()
+
+    def add(self, stage, piece=None):
         found = {}
-        for _, back, slot in self.parts(stage):
-            remote(
-                self.slots.at[slot],
-                self.slots.at[slot],
-                self.sends.at[slot],
-                self.recvs.at[slot],
-                self.place.device(),
-            ).wait_recv()
+        columns = self.columns(piece)
+        for d, back, slot in self.parts(stage):
+            self.copy(stage, d, back, slot, piece).wait_recv()
             found.setdefault(tuple(back), []).append(slot)
         for back, slots in found.items():
             at = self.region(back)
-            total = self.held[at, :].astype(F32)
+            total = self.held[at, columns].astype(F32)
             for slot in slots:
-                total = total + self.slots[slot].astype(F32)
+                total = total + self.slots[slot, :, columns].astype(F32)
             if stage == 0:
-                self.final[...] = total
+                self.final[:, columns] = total
             else:
-                self.held[at, :] = total.astype(BF)
+                self.held[at, columns] = total.astype(BF)
 
     def drain(self):
-        for copy in self.sent:
-            copy.wait_send()
+        for stage, piece in self.sent:
+            for d, back, slot in self.parts(stage):
+                self.copy(stage, d, back, slot, piece).wait_send()
+
+
+class RowScatter(Scatter):
+    def part_q(self, z, p):
+        place = self.place
+        behind = (place.z - z + place.deep) % place.deep
+        return [p, (place.deep - behind) % place.deep, 0], (p * place.deep + behind) * 2
+
+    def copy_q(self, z, p):
+        shifts, slot = self.part_q(z, p)
+        return self.copy(2, 1, shifts, slot, None)
+
+    def send_q(self, z):
+        for p in range(2):
+            self.copy_q(z, p).start()
+
+    def add_q(self, z):
+        for p in range(2):
+            shifts, slot = self.part_q(z, p)
+            self.copy_q(z, p).wait_recv()
+            at = self.region(shifts)
+            self.held[at, :] = (self.held[at, :].astype(F32) + self.slots[slot].astype(F32)).astype(BF)
+
+    def copy_z(self, z, p):
+        place = self.place
+        ahead = (z - place.z + place.deep) % place.deep
+        return self.copy(1, ahead, [p, 0, 0], (p * place.deep + ahead) * 2 - 1, None)
+
+    def send_z(self, z):
+        @pl.when(self.place.z != z)
+        def _():
+            for p in range(2):
+                self.copy_z(z, p).start()
+
+    def drain(self):
+        place = self.place
+        for z in range(place.deep):
+            for p in range(2):
+                self.copy_q(z, p).wait_send()
+        for d, back, slot in self.parts(1):
+            self.copy(1, d, back, slot, None).wait_send()
+        super().drain()
 
 
 def backward_kernel(
@@ -718,12 +950,15 @@
     i_act,
     i_slope,
     i_expon,
+    i_result,
+    i_own_cot,
     o_qkv,
     o_out,
     o_up,
     o_down,
     o_small,
     o_patch,
+    o_result,
     w_qkv,
     w_out,
     w_up,
@@ -785,7 +1020,6 @@
         pltpu.make_async_copy(src, dst, load_sems.at[i])
         for i, (src, dst) in enumerate(
             (
-                (i_cot, upstream),
                 (i_second, second),
                 (i_middle, middle),
                 (i_small, vectors),
@@ -820,24 +1054,47 @@
         )
         return [pltpu.make_async_copy(src, dst, pair_sems.at[slot, n]) for n, (src, dst) in enumerate(moves)]
 
-    for copy in loads[:2] + chunk_loads(0) + loads[2:]:
+    for step in range(sources):
+        source = place.mate(step)
+        at = pl.ds(pl.multiple_of(source * span, span), span)
+        loads.insert(
+            step,
+            pltpu.make_async_copy(
+                i_own_cot.at[place.tm] if step == 0 else i_cot.at[at], upstream.at[at], load_sems.at[6 + step]
+            ),
+        )
+    early = sources + 1
+    for copy in loads[:early] + chunk_loads(0) + loads[early:]:
         copy.start()
     place.enter()
 
+    def result_copy(step):
+        to = place.mate(step)
+        return remote(
+            i_result.at[pl.ds(pl.multiple_of(to * span, span), span)],
+            o_result.at[place.tm],
+            row_sends.at[1, step],
+            row_recvs.at[1, step],
+            (place.batch, to),
+        )
+
+    result_in = pltpu.make_async_copy(
+        i_result.at[pl.ds(pl.multiple_of(place.tm * span, span), span)], patch.at[sources - 1], local_sems.at[5]
+    )
+    result_in.start()
+    result_out = pltpu.make_async_copy(patch.at[sources - 1], o_result.at[place.tm], local_sems.at[5])
+    for step in range(1, sources):
+        result_copy(step).start()
+
     zpq = Route(place, "zpq", True)
-    pzq = Route(place, "pzq", False)
-    scatters = [
-        Scatter(place, route, held, slots, final, scatter_sends.at[i], scatter_recvs.at[i])
-        for i, (route, held, slots, final) in enumerate(
-            (
-                (zpq, h_qkv, s_qkv, f_qkv),
-                (zpq, h_out, s_out, f_out),
-                (zpq, h_up, s_up, f_up),
-                (pzq, h_down, s_down, f_down),
-            )
-        )
-    ]
-    by_qkv, by_out, by_up, by_down = scatters
+    pzq = Route(place, "pzq", True)
+    xzy = Route(place, "pzq", False)
+    zxy = Route(place, "zpq", False)
+    by_qkv = Scatter(place, xzy, h_qkv, s_qkv, f_qkv, scatter_sends.at[0], scatter_recvs.at[0], part)
+    by_out = Scatter(place, zpq, h_out, s_out, f_out, scatter_sends.at[1], scatter_recvs.at[1], part)
+    by_up = Scatter(place, zxy, h_up, s_up, f_up, scatter_sends.at[2], scatter_recvs.at[2], part)
+    by_down = RowScatter(place, pzq, h_down, s_down, f_down, scatter_sends.at[3], scatter_recvs.at[3])
+    scatters = [by_qkv, by_out, by_up, by_down]
 
     def columns(c):
         return pl.ds(pl.multiple_of(c * part, 128), part)
@@ -866,9 +1123,49 @@
     def qkv_chunk(i):
         return (1 + i, h_qkv.at[:, pl.ds(pl.multiple_of(i * part, 128), part)], 2 * chunks + 1 + i)
 
-    out_chunk = (0, h_out, 2 * chunks)
-
-    for copy in loads[:2]:
+    def out_chunk(i):
+        return (0, h_out, 2 * chunks)
+
+    named = {
+        "qkv": (by_qkv, qkv_chunk),
+        "out": (by_out, out_chunk),
+        "up": (by_up, up_chunk),
+        "down": (by_down, down_chunk),
+    }
+    summed = VectorSum(place, small, small_slots, small_sends, small_recvs)
+
+    def run(steps):
+        for what, *which in steps:
+            if what == "vector send":
+                summed.send(which[0])
+            elif what == "vector add":
+                summed.add(which[0])
+            elif what == "turn":
+                by_down.add_q(which[0])
+                by_down.send_z(which[0])
+            elif what == "deliver":
+                deliver(*deliveries[which[0]])
+            elif what == "settle":
+                scatter, chunk = named[which[0]]
+                settle(*chunk(which[1]))
+                if scatter is by_down:
+                    scatter.send_q(which[1])
+                else:
+                    scatter.send(2, which[1])
+            else:
+                scatter = named[which[0]][0]
+                stage = which[1]
+                piece = None if scatter is by_down else which[2]
+                scatter.add(stage, piece)
+                if stage > 0:
+                    scatter.send(stage - 1, piece)
+
+    def after(loop, index=0, part=0, parts=1):
+        for when, steps in BACKWARD_STEPS.get(loop, {}).items():
+            if when % parts == part:
+                pl.when(index == when // parts)(functools.partial(run, steps))
+
+    for copy in loads[:early]:
         copy.wait()
 
     def feed(j):
@@ -885,8 +1182,10 @@
         small[0, pl.ds(9 + j, 1), :] = column_sum(pre_grad.astype(F32))
         staged[down_chunk(j)[0]] = tn(expon[slot, 0, :, 0:width], upstream[...]).astype(BF)
         hand(*down_chunk(j)).start()
+        after("feed", j, 0, 3)
         staged[up_chunk(j)[0]] = tn(second[...], pre_grad).astype(BF)
         hand(*up_chunk(j)).start()
+        after("feed", j, 1, 3)
         grown = nt(pre_grad, w_up[slot])
 
         @pl.when(j == 0)
@@ -896,8 +1195,8 @@
         @pl.when(j > 0)
         def _():
             gathered[...] = gathered[...] + grown
-            settle(*down_chunk(j - 1))
-            settle(*up_chunk(j - 1))
+
+        after("feed", j, 2, 3)
 
     pl.loop(0, chunks)(feed)
     whole_mixed = pltpu.make_async_copy(i_mixed, expon.at[1, 1, :, pl.ds(0, width)], local_sems.at[0])
@@ -906,13 +1205,8 @@
         copy.start()
     load_first = pltpu.make_async_copy(i_first, first, local_sems.at[1])
     load_first.start()
-    for copy in loads[2:]:
+    for copy in loads[early:]:
         copy.wait()
-    settle(*down_chunk(chunks - 1))
-    settle(*up_chunk(chunks - 1))
-    by_down.send(2)
-    by_up.send(2)
-
     for row in (0, 1, 2, 3, 4, 5, 6, 7, 8, 13, 14, 15):
         small[0, row : row + 1, :] = jnp.zeros((1, width), F32)
 
@@ -932,10 +1226,14 @@
         mixed_grad[at, :] = nt(low_total, w_out[...]).astype(BF)
 
     pl.loop(0, sources)(bend)
+    run(BACKWARD_STEPS.get("bend", {}).get(0, []))
     whole_mixed.wait()
     staged[0] = tn(expon[1, 1, :, 0:width], middle[...].astype(BF)).astype(BF)
-    hand(*out_chunk).start()
+    hand(*out_chunk(0)).start()
+    run(BACKWARD_STEPS.get("out", {}).get(0, []))
     load_first.wait()
+    result_in.wait()
+    result_out.start()
 
     lane = lax.broadcasted_iota(jnp.int32, (1, 2 * half), 1)
     low = lane < half
@@ -971,6 +1269,8 @@
             query_grads.append(jnp.concatenate(query_parts, 0))
             key_grads.append(tn(query, score_grad[h]))
             value_grads.append(tn(scaled, expon[slot, h]))
+            if h == 0:
+                after("attend", p, 0, 2)
         query_grad = (jnp.where(low, query_grads[0], query_grads[1]) * (1.0 / math.sqrt(half))).astype(BF)
         key_grad = jnp.concatenate([key_grads[0][:half], key_grads[1][half:]], 0).T.astype(BF)
         value_grad = jnp.concatenate([value_grads[0][:half], value_grads[1][half:]], 0).T.astype(BF)
@@ -996,15 +1296,13 @@
         def _():
             hand(*qkv_chunk(p // 2)).start()
 
+        after("attend", p, 1, 2)
+
     pl.loop(0, pairs)(attend)
     load_x = pltpu.make_async_copy(i_x, expon.at[0, 0, :, pl.ds(0, width)], local_sems.at[2])
     load_x.start()
     load_x.wait()
-    settle(*out_chunk)
-    for i in range(3):
-        settle(*qkv_chunk(i))
-    by_out.send(2)
-    by_qkv.send(2)
+    result_out.wait()
 
     def close(step):
         source = place.mate(sources - 1 - step)
@@ -1026,24 +1324,16 @@
             remote(
                 patch.at[step],
                 o_patch.at[place.tm],
-                row_sends.at[sources - 1 - step],
-                row_recvs.at[sources - 1 - step],
+                row_sends.at[0, sources - 1 - step],
+                row_recvs.at[0, sources - 1 - step],
                 (place.batch, source),
             ).start()
+
+        after("close", step)
 
     pl.loop(0, sources)(close)
     own_patch = pltpu.make_async_copy(patch.at[sources - 1], o_patch.at[place.tm], local_sems.at[3])
     own_patch.start()
-    sum_vectors(place, small, small_slots, small_sends, small_recvs)
-    own_small = pltpu.make_async_copy(small.at[4], o_small, local_sems.at[4])
-    own_small.start()
-    for stage in (2, 1, 0):
-        for scatter in scatters:
-            scatter.add(stage)
-        if stage > 0:
-            for scatter in scatters:
-                scatter.send(stage - 1)
-
     moves = []
 
     def deliver(final, target, pieces):
@@ -1054,7 +1344,7 @@
             theirs = pl.ds(pl.multiple_of((1 - place.c) * shard, 8), shard)
             n = len(moves) // 2
             moves.append(
-                pltpu.make_async_copy(final.at[mine, pl.ds(near, size)], target.at[:, to], local_sems.at[5 + n])
+                pltpu.make_async_copy(final.at[mine, pl.ds(near, size)], target.at[:, to], local_sems.at[6 + n])
             )
             moves.append(
                 remote(
@@ -1068,34 +1358,40 @@
             moves[-2].start()
             moves[-1].start()
 
-    deliver(f_down, o_down, [(0, 0, part, part)])
-    deliver(f_up, o_up, [(j * part, j * width, part, part) for j in range(chunks)])
-    deliver(f_out, o_out, [(0, 0, part, part)])
-    deliver(
-        f_qkv,
-        o_qkv,
-        [
-            (i * part + n * 2 * half, n * width + i * 4 * half, 2 * half, 2 * half)
-            for i in range(3)
-            for n in range(3)
-        ],
-    )
+    deliveries = {
+        "down": (f_down, o_down, [(0, 0, part, part)]),
+        "up": (f_up, o_up, [(j * part, j * width, part, part) for j in range(chunks)]),
+        "out": (f_out, o_out, [(0, 0, part, part)]),
+        "qkv": (
+            f_qkv,
+            o_qkv,
+            [
+                (i * part + n * 2 * half, n * width + i * 4 * half, 2 * half, 2 * half)
+                for i in range(3)
+                for n in range(3)
+            ],
+        ),
+    }
+    run(BACKWARD_STEPS["tail"][0])
+    own_small = pltpu.make_async_copy(small.at[4], o_small, local_sems.at[4])
+    own_small.start()
     for move in moves:
         move.wait()
     for step in range(1, sources):
         copy = remote(
-            patch.at[0], o_patch.at[place.mate(step)], row_sends.at[step], row_recvs.at[step], place.device()
+            patch.at[0], o_patch.at[place.mate(step)], row_sends.at[0, step], row_recvs.at[0, step], place.device()
         )
         copy.wait_recv()
         copy.wait_send()
+        result_copy(step).wait()
     own_patch.wait()
     own_small.wait()
     for scatter in scatters:
         scatter.drain()
 
 
-def backward(deep, saved, shards, patches):
-    sources, span, width = patches.shape
+def backward(deep, saved, shards, cotangent):
+    sources, span, width = cotangent.shape
     rows = sources * span
     chips = deep * 4
     chunks = shards[2].shape[1] // width
@@ -1104,7 +1400,7 @@
     small = saved[4]
     code = saved[7]
     halves = [(2 * chips * s.shape[0], s.shape[1] // 2) for s in shards]
-    outs = [shape(s.shape, F32) for s in shards] + [shape(small.shape, F32), shape(patches.shape, BF)]
+    outs = [shape(s.shape, F32) for s in shards] + [shape(small.shape, F32)] + [shape(cotangent.shape, BF)] * 2
     scratch = [
         pltpu.VMEM(saved[0].shape, BF),
         pltpu.VMEM(saved[1].shape, BF),
@@ -1129,47 +1425,36 @@
         pltpu.VMEM(code.shape, F32),
         pltpu.VMEM((5,) + small.shape, F32),
         pltpu.VMEM((2 + deep,) + small.shape, F32),
-        pltpu.VMEM(patches.shape, BF),
+        pltpu.VMEM(cotangent.shape, BF),
     ]
     dma = pltpu.SemaphoreType.DMA
     scratch += [
-        dma((7,)),
+        dma((6 + sources,)),
         dma((2, 4)),
         dma((2, 6)),
         dma((2 * chunks + 4,)),
         dma((2 * chunks + 4,)),
-        dma((4, chips - 1)),
-        dma((4, chips - 1)),
+        dma((4, chunks, chips - 1)),
+        dma((4, chunks, chips - 1)),
         dma((11 + chunks,)),
         dma((11 + chunks,)),
         dma((2 + deep,)),
         dma((2 + deep,)),
-        dma((sources,)),
-        dma((sources,)),
-        dma((16 + chunks,)),
+        dma((2, sources)),
+        dma((2, sources)),
+        dma((17 + chunks,)),
     ]
     return pl.pallas_call(
         functools.partial(backward_kernel, deep),
         out_shape=outs,
-        in_specs=[HBM] * len(saved),
+        in_specs=[HBM] * (len(saved) + 1),
         out_specs=[HBM] * len(outs),
         scratch_shapes=scratch,
         compiler_params=pltpu.CompilerParams(
             collective_id=1, has_side_effects=True, vmem_limit_bytes=63 * 2**20
         ),
         name="backward",
-    )(*saved)
-
-
-def pack(deep, mask_embed, norm_gain, norm_shift, qv_bias, branch_bias, up_bias, width):
-    device = lax.axis_index("batch") * 4 + lax.axis_index("tm")
-    lines = jnp.concatenate([mask_embed[None], norm_gain, norm_shift, qv_bias, branch_bias], 0)
-    lines = lines.astype(BF).astype(F32)
-    top = lax.dynamic_update_slice(jnp.zeros((9, width), F32), lines, (0, device * lines.shape[1]))
-    flat = lax.dynamic_update_slice(
-        jnp.zeros((7 * width,), F32), up_bias.astype(BF).astype(F32), (device * up_bias.shape[0],)
-    )
-    return jnp.concatenate([top, flat.reshape(7, width)], 0)
+    )(*saved, cotangent)
 
 
 def by_rows(
@@ -1194,13 +1479,13 @@
     lane = 128
     code = jnp.concatenate([mask_flags.reshape(sources, -1, lane), segment_ids.reshape(sources, -1, lane)], 1)
     code = jnp.pad(code.astype(F32), ((0, 0), (0, 8 - code.shape[1]), (0, 0)))
-    small = pack(deep, mask_embed, norm_gain, norm_shift, qv_bias, branch_bias, up_bias, width)
-    *saved, result = forward(deep, patches, cotangent, code, small, *shards)
-    *grads, sums, patch_grad = backward(deep, saved, shards, patches)
+    vector = gather_vectors(mask_embed, norm_gain, norm_shift, qv_bias, branch_bias, up_bias)
+    saved = forward(deep, patches, cotangent, code, vector, *shards)
+    *grads, sums, patch_grad, result = backward(deep, saved, shards, cotangent)
     device = lax.axis_index("batch") * 4 + lax.axis_index("tm")
     piece = mask_embed.shape[0]
     own = lax.dynamic_slice(sums, (0, device * piece), (9, piece))
-    up_sum = lax.dynamic_slice(sums[9:].reshape(-1), (device * up_bias.shape[0],), up_bias.shape)
+    up_sum = lax.dynamic_slice(sums[9:13].reshape(-1), (device * up_bias.shape[0],), up_bias.shape)
     return (
         result.astype(F32),
         patch_grad.astype(F32),

time: 333 us -> 244 us (0.73)
  Pallas kernels: 314 us -> 224 us
  other arithmetic: 10.2 us -> 6.01 us
  local copies, waits for them, and re-layouts: 7.08 us -> 11.1 us
    pallas_call x1, Pallas kernels: 166 us -> 117 us  [backward(): pl.pallas_call(functools.partial(backward_kernel, deep), out_shape=outs,...]
    pallas_call x1, Pallas kernels: 148 us -> 108 us  [forward(): pl.pallas_call(functools.partial(forward_kernel, deep), out_shape=outs, i...]
where the time goes in v2:
time: 244 us; the launch traced here: 242 us
  Pallas kernels  224 us (92%)
  local copies, waits for them, and re-layouts  11.1 us (5%)
  other arithmetic  6.01 us (2%)
    pallas_call x1, Pallas kernels, backward(): pl.pallas_call(functools.partial(backward_kernel, deep), out_shape=outs,...  117 us
    pallas_call x1, Pallas kernels, forward(): pl.pallas_call(functools.partial(forward_kernel, deep), out_shape=outs, i...  108 us

profile of v2, /device:TPU:11, one launch (start us, length us, event | category | flops | bytes accessed | tf_op | source)
XLA Modules:
  0.0 242.1 jit_solution(7527573518453895193)
XLA Ops:
  0.6 1.5 concatenate.13
  2.2 0.7 pad_bitcast_fusion
  2.8 0.6 pad_maximum_fusion.shard_vector
  3.4 0.7 reshape.33
  4.1 0.7 reshape.34
  4.9 0.6 pad.16.code_in
  5.5 107.6 %forward.1 = (bf16[768,2304]{1,0:T(8,128)(2,1)}, bf16[768,768]{1,0:T(8,128)(2,1)}, bf16[768,3072]{1,0:T(8,128)(2,1)}, bf16[3072,768]{1,0:T(8,128)(2,1)}, f32[16,...) custom-call(bf16[4,256,768]{2,1,0:T(8,128)(2,1)} %patches.1, ...), custom_call_target="tpu_custom_call" | custom-call | tf_op jit(solution)/shard_map/forward/pallas_call | solution.py:812
  113.1 116.7 %backward.1 = (f32[24,2304]{1,0:T(8,128)}, f32[24,768]{1,0:T(8,128)}, f32[24,3072]{1,0:T(8,128)}, f32[96,768]{1,0:T(8,128)}, f32[16,768]{1,0:T(8,128)}, /*index=...) custom-call(bf16[768,2304]{1,0:T(8,128)(2,1)} %get-tuple-element.39.i_qkv, bf16[768,768]{1,0:T(8,128)(2,1)} %get-tuple-element.40.i_out, ...), custom_call_target="tpu_custom_call" | custom-call | tf_op jit(solution)/shard_map/backward/pallas_call | solution.py:1447
  229.8 0.0 copy-start
  229.8 3.5 %convert_element_type.18 = f32[4,256,768]{2,1,0:T(8,128)} convert(bf16[4,256,768]{2,1,0:T(8,128)(2,1)} %get-tuple-element.59) | non-fusion elementwise | flops 786432 | bytes 4718592 | tf_op jit(solution)/shard_map/convert_element_type | solution.py:1490
  233.2 0.0 copy-done
  233.3 0.0 copy-start.1
  233.3 1.9 convert_element_type.19
  235.2 0.7 slice.31
  236.0 0.6 dynamic_slice.7
  236.5 1.5 fusion
  238.0 1.3 dynamic-slice_bitcast_fusion
  239.3 0.0 copy-done.3
  239.3 0.7 copy.30
  240.0 0.0 copy-done.4
  240.0 0.6 copy.31
  240.6 0.0 copy-done.2
  240.6 0.7 copy.32
  241.4 0.7 copy.33
  (8 shorter events, 0.0 us)
Async XLA Ops:
  229.8 3.5 %copy-start = (bf16[4,256,768]{2,1,0:T(8,128)(2,1)S(1)}, bf16[4,256,768]{2,1,0:T(8,128)(2,1)}, u32[]{:S(2)}) copy-start(bf16[4,256,768]{2,1,0:T(8,128)(2,1)} %get-tuple-element.60) | copy-start | bytes 4718596
  233.2 6.1 %copy-start.3 = (f32[24,2304]{1,0:T(8,128)S(1)}, f32[24,2304]{1,0:T(8,128)}, u32[]{:S(2)}) copy-start(f32[24,2304]{1,0:T(8,128)} %get-tuple-element.89) | copy-start | bytes 663556
  233.2 6.8 %copy-start.4 = (f32[24,768]{1,0:T(8,128)S(1)}, f32[24,768]{1,0:T(8,128)}, u32[]{:S(2)}) copy-start(f32[24,768]{1,0:T(8,128)} %get-tuple-element.91) | copy-start | bytes 221188
  233.2 7.4 %copy-start.2 = (f32[24,3072]{1,0:T(8,128)S(1)}, f32[24,3072]{1,0:T(8,128)}, u32[]{:S(2)}) copy-start(f32[24,3072]{1,0:T(8,128)} %get-tuple-element.93) | copy-start | bytes 884740
  233.3 8.1 %copy-start.1 = (f32[96,768]{1,0:T(8,128)S(1)}, f32[96,768]{1,0:T(8,128)}, u32[]{:S(2)}) copy-start(f32[96,768]{1,0:T(8,128)} %get-tuple-element.95) | copy-start | bytes 884740

commit v3 on v2

--- a/solution.py
+++ b/solution.py
@@ -17,7 +17,7 @@
 MESH = pl.DeviceIdType.MESH
 HBM = pl.BlockSpec(memory_space=pl.ANY)
 SLOPE = 0.36
-TAIL = (
+COEFFICIENTS = (
     0.14371305209487725,
     0.14177235930704382,
     0.1397197719471602,
@@ -28,169 +28,163 @@
 )
 
 
+VECTOR, QKV, OUT, UP, DOWN = range(5)
+START, PROJECT, ATTEND, RISE, FALL, FEED, BEND, MIX, CLOSE, TAIL = range(10)
+FIRST, STAGE, FINISH, ROWS, COTANGENT, SPREAD = range(6)
+SETTLE, TURN, ADD, VECTOR_SEND, VECTOR_ADD, DELIVER = range(6)
+
 FORWARD_STEPS = {
-    "start": {
+    START: {
         0: [
-            ("first", "vector"),
-            ("first", "qkv"),
-            ("first", "out"),
-            ("first", "up"),
-            (0, "vector", 0, 3),
-            (0, "qkv", 0, 3),
-            (0, "out", 0, 3),
-            (1, "vector", 0, 4),
-            (1, "qkv", 0, 2),
-            (1, "qkv", 2, 4),
-            ("rows",),
-            ("first", "down"),
-            (2, "vector", 0, 8),
-            (1, "out", 0, 2),
-            (1, "out", 2, 4),
-            ("finish", "vector"),
-            (2, "qkv", 0, 4),
-            ("spread",),
-            (2, "qkv", 4, 8),
-            ("finish", "qkv"),
+            (FIRST, VECTOR),
+            (FIRST, QKV),
+            (STAGE, VECTOR, 0, 0, 3),
+            (FIRST, OUT),
+            (FIRST, UP),
+            (STAGE, QKV, 0, 0, 3),
+            (STAGE, VECTOR, 1, 0, 4),
+            (STAGE, QKV, 1, 0, 4),
+            (ROWS,),
+            (STAGE, VECTOR, 2, 0, 8),
+            (FINISH, VECTOR),
+            (STAGE, QKV, 2, 0, 4),
+            (STAGE, OUT, 0, 0, 3),
+            (STAGE, QKV, 2, 4, 8),
+            (SPREAD,),
+            (FIRST, DOWN),
+            (FINISH, QKV),
         ],
     },
-    "project": {
+    PROJECT: {
+        1: [
+            (STAGE, UP, 0, 0, 3),
+        ],
+    },
+    ATTEND: {
+        0: [
+            (STAGE, OUT, 1, 0, 4),
+        ],
+        1: [
+            (STAGE, UP, 1, 0, 4),
+            (STAGE, DOWN, 0, 0, 1),
+        ],
+        3: [
+            (STAGE, DOWN, 1, 0, 3),
+            (STAGE, OUT, 2, 0, 4),
+        ],
+        4: [
+            (STAGE, UP, 2, 0, 4),
+            (STAGE, OUT, 2, 4, 8),
+            (STAGE, UP, 2, 4, 8),
+        ],
+        5: [
+            (FINISH, UP),
+            (FINISH, OUT),
+            (STAGE, DOWN, 1, 3, 6),
+        ],
+    },
+    RISE: {
+        0: [
+            (COTANGENT,),
+            (STAGE, DOWN, 2, 0, 4),
+        ],
+        1: [
+            (STAGE, DOWN, 2, 4, 8),
+        ],
         2: [
-            (0, "up", 0, 3),
-        ],
-    },
-    "attend": {
-        0: [
-            (0, "down", 0, 1),
-        ],
-        2: [
-            (2, "out", 0, 4),
-            (2, "out", 4, 8),
-        ],
-        3: [
-            ("finish", "out"),
-            (1, "up", 0, 2),
-        ],
-        5: [
-            (1, "up", 2, 4),
-            (1, "down", 0, 3),
-        ],
-        8: [
-            (1, "down", 3, 6),
-            (2, "up", 0, 4),
-        ],
-        9: [
-            (2, "up", 4, 8),
-        ],
-        10: [
-            ("finish", "up"),
-            ("cotangent",),
-        ],
-    },
-    "rise": {
-        1: [
-            (2, "down", 0, 4),
-        ],
-        2: [
-            (2, "down", 4, 8),
-        ],
-        3: [
-            ("finish", "down"),
+            (FINISH, DOWN),
         ],
     },
 }
 
 
 BACKWARD_STEPS = {
-    "feed": {
+    FEED: {
+        0: [
+            (SETTLE, DOWN, 0),
+            (SETTLE, UP, 0),
+        ],
+        1: [
+            (SETTLE, DOWN, 1),
+        ],
         2: [
-            ("settle", "up", 0),
-        ],
-        5: [
-            ("settle", "down", 0),
-        ],
-        6: [
-            ("settle", "down", 1),
-        ],
-        7: [
-            ("turn", 0),
-            ("settle", "up", 1),
-            ("settle", "down", 2),
-        ],
-        9: [
-            ("turn", 1),
-            ("add", "up", 2, 0),
-        ],
-        11: [
-            ("turn", 2),
-            ("settle", "down", 3),
-            ("settle", "up", 2),
+            (SETTLE, UP, 1),
+            (SETTLE, DOWN, 2),
+            (TURN, 0),
+        ],
+        3: [
+            (TURN, 1),
+            (SETTLE, DOWN, 3),
+            (TURN, 2),
+            (SETTLE, UP, 3),
         ],
     },
-    "attend": {
+    MIX: {
+        0: [
+            (SETTLE, UP, 2),
+            (TURN, 3),
+        ],
+    },
+    ATTEND: {
         1: [
-            ("turn", 3),
-            ("settle", "up", 3),
+            (ADD, UP, 2, 0),
+            (SETTLE, OUT, 0),
+            (ADD, UP, 2, 2),
+            (ADD, UP, 2, 3),
+        ],
+        2: [
+            (ADD, UP, 2, 1),
+        ],
+        3: [
+            (ADD, OUT, 2, 0),
+            (ADD, UP, 1, 2),
+            (ADD, UP, 1, 1),
+            (ADD, UP, 1, 3),
         ],
         4: [
-            ("settle", "out", 0),
-        ],
-        6: [
-            ("add", "up", 2, 3),
-            ("add", "up", 2, 1),
-            ("add", "up", 1, 0),
-            ("settle", "qkv", 0),
-        ],
-        8: [
-            ("add", "up", 1, 1),
-            ("add", "out", 2, 0),
-            ("add", "qkv", 2, 0),
-            ("add", "up", 1, 3),
-        ],
-        9: [
-            ("add", "up", 2, 2),
-        ],
-        10: [
-            ("add", "out", 1, 0),
-            ("add", "down", 1, 0),
+            (SETTLE, QKV, 0),
+            (ADD, OUT, 1, 0),
+            (ADD, DOWN, 1, 0),
+            (ADD, UP, 1, 0),
         ],
     },
-    "close": {
+    CLOSE: {
+        1: [
+            (ADD, OUT, 0, 0),
+            (ADD, QKV, 2, 0),
+            (ADD, UP, 0, 2),
+            (ADD, UP, 0, 1),
+        ],
+        2: [
+            (SETTLE, QKV, 1),
+        ],
+    },
+    TAIL: {
         0: [
-            ("settle", "qkv", 2),
-        ],
-        1: [
-            ("add", "down", 0, 0),
-        ],
-    },
-    "tail": {
-        0: [
-            ("add", "up", 1, 2),
-            ("add", "up", 0, 0),
-            ("add", "up", 0, 1),
-            ("add", "qkv", 2, 2),
-            ("vector send", 0),
-            ("add", "out", 0, 0),
-            ("settle", "qkv", 1),
-            ("vector add", 0),
-            ("deliver", "out"),
-            ("add", "qkv", 2, 1),
-            ("vector send", 1),
-            ("add", "qkv", 1, 0),
-            ("add", "up", 0, 2),
-            ("deliver", "down"),
-            ("add", "qkv", 1, 2),
-            ("add", "up", 0, 3),
-            ("deliver", "up"),
-            ("vector add", 1),
-            ("add", "qkv", 0, 0),
-            ("vector send", 2),
-            ("vector add", 2),
-            ("vector send", 3),
-            ("add", "qkv", 1, 1),
-            ("add", "qkv", 0, 2),
-            ("add", "qkv", 0, 1),
-            ("deliver", "qkv"),
-            ("vector add", 3),
+            (VECTOR_SEND, 0),
+            (DELIVER, OUT),
+            (ADD, DOWN, 0, 0),
+            (ADD, QKV, 2, 1),
+            (VECTOR_ADD, 0),
+            (ADD, UP, 0, 3),
+            (SETTLE, QKV, 2),
+            (ADD, QKV, 2, 2),
+            (VECTOR_SEND, 1),
+            (ADD, UP, 0, 0),
+            (ADD, QKV, 1, 0),
+            (DELIVER, DOWN),
+            (VECTOR_ADD, 1),
+            (VECTOR_SEND, 2),
+            (VECTOR_ADD, 2),
+            (VECTOR_SEND, 3),
+            (ADD, QKV, 1, 2),
+            (ADD, QKV, 1, 1),
+            (ADD, QKV, 0, 2),
+            (ADD, QKV, 0, 0),
+            (DELIVER, UP),
+            (ADD, QKV, 0, 1),
+            (DELIVER, QKV),
+            (VECTOR_ADD, 3),
         ],
     },
 }
@@ -211,8 +205,8 @@
 def gelu_and_slope(pre):
     size = jnp.abs(pre)
     t = 1.0 / (1.0 + SLOPE * size)
-    poly = jnp.full_like(t, TAIL[-1])
-    for term in TAIL[-2::-1]:
+    poly = jnp.full_like(t, COEFFICIENTS[-1])
+    for term in COEFFICIENTS[-2::-1]:
         poly = poly * t + term
     bell = jnp.exp2(pre * pre * (-0.5 * LOG2E))
     lower = poly * t * bell
@@ -315,7 +309,7 @@
         self.shard, self.joined, self.full = shard, joined, full
         self.local, self.sends, self.recvs = local, sends, recvs
         self.rows = shard.shape[0]
-        self.half = shard.shape[1] // 2
+        self.half = joined.shape[1]
         self.count = 0
 
     def columns(self, c):
@@ -431,11 +425,16 @@
         self.held[stage + 1] = total
 
 
-def gather_vectors(mask_embed, norm_gain, norm_shift, qv_bias, branch_bias, up_bias):
-    lines = jnp.concatenate([mask_embed[None], norm_gain, norm_shift, qv_bias, branch_bias], 0)
-    lines = jnp.pad(lines, ((0, 0), (0, 128 - lines.shape[1])))
-    rest = jnp.concatenate([lines[8:], jnp.pad(up_bias, (0, 128 - up_bias.shape[0]))[None]], 0)
-    return jnp.concatenate([lines[:8], jnp.pad(rest, ((0, 6), (0, 0)))], 1)
+def fill_vectors(block, mask_embed, norm_gain, norm_shift, qv_bias, branch_bias, up_bias):
+    block[...] = jnp.zeros_like(block)
+    piece = mask_embed.shape[1]
+    row = 0
+    for part in (mask_embed, norm_gain, norm_shift, qv_bias):
+        block[row : row + part.shape[0], 0:piece] = part[...]
+        row += part.shape[0]
+    block[row : row + 1, 0:piece] = branch_bias[0:1, :]
+    block[0:1, 128 : 128 + piece] = branch_bias[1:2, :]
+    block[1:2, 128 : 128 + up_bias.shape[1]] = up_bias[...]
 
 
 def spread_vectors(blocks, vectors):
@@ -459,19 +458,24 @@
         put(block[1:2, 128:], slice(9 + up // width, 10 + up // width), up % width)
 
 
-def code_columns(code, source):
-    turned = jnp.transpose(code[source])
-    flags = jnp.concatenate([turned[:, 0:1], turned[:, 1:2]], 0)
-    clips = jnp.concatenate([turned[:, 2:3], turned[:, 3:4]], 0)
-    return flags, clips
+def column_of(table, source, row):
+    line = table[source, pl.ds(row, 1), :].astype(F32)
+    tall = jnp.broadcast_to(line, (8, line.shape[1]))
+    return jnp.concatenate([tall[:, n : n + 128].T[:, 0:1] for n in range(0, line.shape[1], 128)], 0)
 
 
 def forward_kernel(
     deep,
     patches,
     cotangent,
-    code_in,
-    shard_vector,
+    flags_in,
+    clips_in,
+    mask_embed,
+    norm_gain,
+    norm_shift,
+    qv_bias,
+    branch_bias,
+    up_bias,
     shard_qkv,
     shard_out,
     shard_up,
@@ -483,7 +487,7 @@
     o_small,
     o_x,
     o_cot,
-    o_code,
+    o_flags,
     o_first,
     o_q,
     o_k,
@@ -505,10 +509,12 @@
     j_up,
     j_down,
     j_vector,
+    shard_vector,
     w_vector,
     small,
     x,
-    code,
+    flags_all,
+    clips_all,
     first,
     q,
     k,
@@ -540,26 +546,38 @@
     inner = w_up.shape[1]
     chunks = inner // width
 
+    fill_vectors(shard_vector, mask_embed, norm_gain, norm_shift, qv_bias, branch_bias, up_bias)
     place.enter()
 
-    kinds = ((patches, x), (code_in, code), (cotangent, o_cot))
+    kinds = ((patches, x), (flags_in, flags_all), (clips_in, clips_all), (cotangent, o_cot))
+
+    def landing(kind, source):
+        dst = kinds[kind][1]
+        if kind in (1, 2):
+            return dst.at[source]
+        return dst.at[pl.ds(pl.multiple_of(source * span, span), span)]
+
+    def leaving(kind, to):
+        src = kinds[kind][0]
+        return src if kind in (1, 2) else src.at[to]
 
     def own_part(kind):
-        src, dst = kinds[kind]
-        to = dst.at[pl.ds(pl.multiple_of(place.tm * span, span), span)] if kind != 1 else dst.at[place.tm]
-        return pltpu.make_async_copy(src.at[place.tm], to, local_sems.at[1 + kind])
+        return pltpu.make_async_copy(
+            leaving(kind, place.tm), landing(kind, place.tm), local_sems.at[kind]
+        )
 
     def row_copy(kind, step, to):
-        src, dst = kinds[kind]
-        here = dst.at[pl.ds(pl.multiple_of(place.tm * span, span), span)] if kind != 1 else dst.at[place.tm]
         return remote(
-            src.at[to], here, row_sends.at[kind, step], row_recvs.at[kind, step], (place.batch, to)
+            leaving(kind, to),
+            landing(kind, place.tm),
+            row_sends.at[kind, step],
+            row_recvs.at[kind, step],
+            (place.batch, to),
         )
 
     def row_wait(kind, step):
-        src, dst = kinds[kind]
         source = place.mate(step)
-        there = dst.at[pl.ds(pl.multiple_of(source * span, span), span)] if kind != 1 else dst.at[source]
+        there = landing(kind, source)
         remote(
             there, there, row_sends.at[kind, step], row_recvs.at[kind, step], (place.batch, source)
         ).wait_recv()
@@ -567,22 +585,23 @@
     zpq = Route(place, "zpq", True)
     zxy = Route(place, "zpq", False)
     pzq = Route(place, "pzq", True)
-    gathers = [
-        Gather(place, route, shard, joined, full, join_sems.at[i], gather_sends.at[i], gather_recvs.at[i])
-        for i, (route, shard, joined, full) in enumerate(
-            (
-                (zpq, shard_vector, j_vector, w_vector),
-                (zxy, shard_qkv, j_qkv, w_qkv),
-                (zxy, shard_out, j_out, w_out),
-                (zpq, shard_up, j_up, w_up),
-                (pzq, shard_down, j_down, w_down),
-            )
-        )
-    ]
+    xzy = Route(place, "pzq", False)
+    named = {}
+    for i, (name, route, shard, joined, full) in enumerate(
+        (
+            (VECTOR, zpq, shard_vector, j_vector, w_vector),
+            (QKV, zxy, shard_qkv, j_qkv, w_qkv),
+            (OUT, zxy, shard_out, j_out, w_out),
+            (UP, zpq, shard_up, j_up, w_up),
+            (DOWN, pzq, shard_down, j_down, w_down),
+        )
+    ):
+        named[name] = Gather(
+            place, route, shard, joined, full, join_sems.at[i], gather_sends.at[i], gather_recvs.at[i]
+        )
+    gathers = list(named.values())
     for gather in gathers:
         gather.join()
-    named = dict(zip(("vector", "qkv", "out", "up", "down"), gathers))
-
     def send_rows(kinds):
         for kind in kinds:
             for step in range(1, sources):
@@ -590,27 +609,30 @@
 
     def run(steps):
         for what, *which in steps:
-            if what == "rows":
-                send_rows((1, 0))
-            elif what == "cotangent":
-                send_rows((2,))
-            elif what == "spread":
+            if what == ROWS:
+                send_rows((1, 2, 0))
+            elif what == COTANGENT:
+                send_rows((3,))
+            elif what == SPREAD:
                 spread_vectors(w_vector, small)
-            elif what == "first":
+            elif what == FIRST:
                 named[which[0]].first()
-            elif what == "finish":
+            elif what == FINISH:
                 named[which[0]].finish()
             else:
-                named[which[0]].stage(what, slice(which[1], which[2]))
-
-    def after(loop, index, part=0, parts=1):
+                named[which[0]].stage(which[1], slice(which[2], which[3]))
+
+    def after(loop, index):
         for when, steps in FORWARD_STEPS.get(loop, {}).items():
-            if when % parts == part:
-                pl.when(index == when // parts)(functools.partial(run, steps))
-
-    for kind in (1, 0):
+            if isinstance(index, int):
+                if index == when:
+                    run(steps)
+            else:
+                pl.when(index == when)(functools.partial(run, steps))
+
+    for kind in (1, 2, 0):
         own_part(kind).start()
-    run(FORWARD_STEPS["start"][0])
+    run(FORWARD_STEPS[START][0])
     keeping = []
 
     def keep(src, dst):
@@ -618,27 +640,26 @@
         copy.start()
         keeping.append(copy)
 
-    keep(w_qkv, o_qkv)
-    keep(small, o_small)
 
     vectors = small
     lane = lax.broadcasted_iota(jnp.int32, (1, 2 * half), 1)
     low = lane < half
     own_lanes = [low.astype(F32), 1.0 - low.astype(F32)]
 
-    for kind in (1, 0):
+    for kind in (1, 2, 0):
         own_part(kind).wait()
 
     @pl.loop(0, sources)
     def _(step):
         @pl.when(step > 0)
         def _():
-            row_wait(1, step)
-            row_wait(0, step)
+            for kind in (1, 2, 0):
+                row_wait(kind, step)
 
         source = place.mate(step)
         at = pl.ds(pl.multiple_of(source * span, span), span)
-        flags, clips = code_columns(code, source)
+        flags = column_of(flags_all, source, place.tm)
+        clips = column_of(clips_all, source, place.tm)
         start = jnp.where(flags == 1.0, vectors[0:1, :], x[at, :].astype(F32))
         middle[at, :] = start
         center, speed = moments(start)
@@ -654,9 +675,9 @@
             coded = jnp.logical_and(clip_lane >= base, clip_lane < base + 5.0)
             q_code[h, at, :] = jnp.where(same, 1.0, 0.0).astype(BF)
             k_code[h, at, :] = jnp.where(jnp.logical_and(coded, jnp.logical_not(same)), FAR, 0.0).astype(BF)
-        after("project", step)
-
-    for src, dst in ((x, o_x), (code, o_code), (first, o_first), (q, o_q), (k, o_k), (v, o_v)):
+        after(PROJECT, step)
+
+    for src, dst in ((w_qkv, o_qkv), (small, o_small), (x, o_x), (flags_all, o_flags), (first, o_first), (q, o_q), (k, o_k), (v, o_v)):
         keep(src, dst)
 
     block = min(rows, 512)
@@ -692,9 +713,8 @@
             speed = 1.0 / totals
             rate[at, lanes] = speed
             mixed[at, lanes] = (top * speed).astype(BF)
-            if part == rows // block - 1:
-                expon_copy(p).start()
-            after("attend", p, part, rows // block)
+        expon_copy(p).start()
+        after(ATTEND, p)
 
     pl.loop(0, pairs)(attend)
     for src, dst in ((w_out, o_out), (w_up, o_up), (mixed, o_mixed), (rate, o_rate)):
@@ -735,7 +755,7 @@
             slope[step % 2, j] = steep.astype(BF)
         for copy in slope_copies(step) + act_copies(step):
             copy.start()
-        after("rise", step)
+        after(RISE, step)
 
     def fall(step):
         at = pl.ds(pl.multiple_of(step * span, span), span)
@@ -757,8 +777,8 @@
         for copy in slope_copies(step):
             copy.wait()
     for step in range(1, sources):
-        row_wait(2, step)
-        for kind in (0, 1, 2):
+        row_wait(3, step)
+        for kind in range(4):
             row_copy(kind, step, place.mate(step)).wait_send()
     for copy in keeping:
         copy.wait()
@@ -766,29 +786,32 @@
         gather.drain()
 
 
-def forward(deep, patches, cotangent, code, vector, qkv, out, up, down):
+def forward(deep, patches, cotangent, flags, clips, vectors, shards):
     sources, span, width = patches.shape
+    qkv, out, up, down = shards
     rows = sources * span
     chips = deep * 4
     inner = up.shape[1]
     chunks = inner // width
     shape = jax.ShapeDtypeStruct
-    shards = (qkv, out, up, down)
     fulls = [(2 * chips * s.shape[0], s.shape[1]) for s in shards]
     plane = (rows, width)
     outs = [shape(f, BF) for f in fulls]
-    outs += [shape((16, width), F32), shape(plane, BF), shape(plane, BF), shape(code.shape, F32)]
+    outs += [shape((16, width), F32), shape(plane, BF), shape(plane, BF)]
+    outs += [shape((sources,) + flags.shape, jnp.int32)]
     outs += [shape(plane, BF)] * 6 + [shape(plane, F32)] * 2
     outs += [shape((chunks, rows, width), BF)] * 2
     outs += [shape((HEADS, rows, rows), BF), shape(plane, BF)]
     scratch = [pltpu.VMEM(f, BF) for f in fulls]
     scratch += [pltpu.VMEM((2 * s.shape[0], s.shape[1] // 2), F32) for s in shards]
     scratch += [
-        pltpu.VMEM((16, vector.shape[1] // 2), F32),
-        pltpu.VMEM((16 * chips, vector.shape[1]), BF),
+        pltpu.VMEM((16, 128), F32),
+        pltpu.VMEM((8, 256), F32),
+        pltpu.VMEM((16 * chips, 256), BF),
         pltpu.VMEM((16, width), F32),
         pltpu.VMEM(plane, BF),
-        pltpu.VMEM(code.shape, F32),
+        pltpu.VMEM((sources,) + flags.shape, jnp.int32),
+        pltpu.VMEM((sources,) + flags.shape, jnp.int32),
     ]
     scratch += [pltpu.VMEM(plane, BF)] * 6 + [pltpu.VMEM(plane, F32)] * 2
     scratch += [
@@ -812,14 +835,14 @@
     return pl.pallas_call(
         functools.partial(forward_kernel, deep),
         out_shape=outs,
-        in_specs=[HBM] * 8,
+        in_specs=[HBM] * 4 + [pl.BlockSpec(memory_space=pltpu.VMEM)] * 6 + [HBM] * 4,
         out_specs=[HBM] * len(outs),
         scratch_shapes=scratch,
         compiler_params=pltpu.CompilerParams(
             collective_id=0, has_side_effects=True, vmem_limit_bytes=62 * 2**20
         ),
         name="forward",
-    )(patches, cotangent, code, vector, qkv, out, up, down)
+    )(patches, cotangent, flags, clips, *vectors, *shards)
 
 
 class Scatter:
@@ -938,7 +961,7 @@
     i_small,
     i_x,
     i_cot,
-    i_code,
+    i_flags,
     i_first,
     i_q,
     i_k,
@@ -986,7 +1009,7 @@
     f_up,
     f_down,
     vectors,
-    code,
+    flags_all,
     small,
     small_slots,
     patch,
@@ -1023,7 +1046,7 @@
                 (i_second, second),
                 (i_middle, middle),
                 (i_small, vectors),
-                (i_code, code),
+                (i_flags, flags_all),
                 (i_out, w_out),
                 (i_qkv, w_qkv),
             )
@@ -1091,8 +1114,8 @@
     xzy = Route(place, "pzq", False)
     zxy = Route(place, "zpq", False)
     by_qkv = Scatter(place, xzy, h_qkv, s_qkv, f_qkv, scatter_sends.at[0], scatter_recvs.at[0], part)
-    by_out = Scatter(place, zpq, h_out, s_out, f_out, scatter_sends.at[1], scatter_recvs.at[1], part)
-    by_up = Scatter(place, zxy, h_up, s_up, f_up, scatter_sends.at[2], scatter_recvs.at[2], part)
+    by_out = Scatter(place, zxy, h_out, s_out, f_out, scatter_sends.at[1], scatter_recvs.at[1], part)
+    by_up = Scatter(place, zpq, h_up, s_up, f_up, scatter_sends.at[2], scatter_recvs.at[2], part)
     by_down = RowScatter(place, pzq, h_down, s_down, f_down, scatter_sends.at[3], scatter_recvs.at[3])
     scatters = [by_qkv, by_out, by_up, by_down]
 
@@ -1127,25 +1150,25 @@
         return (0, h_out, 2 * chunks)
 
     named = {
-        "qkv": (by_qkv, qkv_chunk),
-        "out": (by_out, out_chunk),
-        "up": (by_up, up_chunk),
-        "down": (by_down, down_chunk),
+        QKV: (by_qkv, qkv_chunk),
+        OUT: (by_out, out_chunk),
+        UP: (by_up, up_chunk),
+        DOWN: (by_down, down_chunk),
     }
     summed = VectorSum(place, small, small_slots, small_sends, small_recvs)
 
     def run(steps):
         for what, *which in steps:
-            if what == "vector send":
+            if what == VECTOR_SEND:
                 summed.send(which[0])
-            elif what == "vector add":
+            elif what == VECTOR_ADD:
                 summed.add(which[0])
-            elif what == "turn":
+            elif what == TURN:
                 by_down.add_q(which[0])
                 by_down.send_z(which[0])
-            elif what == "deliver":
+            elif what == DELIVER:
                 deliver(*deliveries[which[0]])
-            elif what == "settle":
+            elif what == SETTLE:
                 scatter, chunk = named[which[0]]
                 settle(*chunk(which[1]))
                 if scatter is by_down:
@@ -1160,10 +1183,13 @@
                 if stage > 0:
                     scatter.send(stage - 1, piece)
 
-    def after(loop, index=0, part=0, parts=1):
+    def after(loop, index):
         for when, steps in BACKWARD_STEPS.get(loop, {}).items():
-            if when % parts == part:
-                pl.when(index == when // parts)(functools.partial(run, steps))
+            if isinstance(index, int):
+                if index == when:
+                    run(steps)
+            else:
+                pl.when(index == when)(functools.partial(run, steps))
 
     for copy in loads[:early]:
         copy.wait()
@@ -1182,10 +1208,8 @@
         small[0, pl.ds(9 + j, 1), :] = column_sum(pre_grad.astype(F32))
         staged[down_chunk(j)[0]] = tn(expon[slot, 0, :, 0:width], upstream[...]).astype(BF)
         hand(*down_chunk(j)).start()
-        after("feed", j, 0, 3)
         staged[up_chunk(j)[0]] = tn(second[...], pre_grad).astype(BF)
         hand(*up_chunk(j)).start()
-        after("feed", j, 1, 3)
         grown = nt(pre_grad, w_up[slot])
 
         @pl.when(j == 0)
@@ -1196,7 +1220,7 @@
         def _():
             gathered[...] = gathered[...] + grown
 
-        after("feed", j, 2, 3)
+        after(FEED, j)
 
     pl.loop(0, chunks)(feed)
     whole_mixed = pltpu.make_async_copy(i_mixed, expon.at[1, 1, :, pl.ds(0, width)], local_sems.at[0])
@@ -1226,11 +1250,11 @@
         mixed_grad[at, :] = nt(low_total, w_out[...]).astype(BF)
 
     pl.loop(0, sources)(bend)
-    run(BACKWARD_STEPS.get("bend", {}).get(0, []))
+    after(BEND, 0)
     whole_mixed.wait()
     staged[0] = tn(expon[1, 1, :, 0:width], middle[...].astype(BF)).astype(BF)
     hand(*out_chunk(0)).start()
-    run(BACKWARD_STEPS.get("out", {}).get(0, []))
+    after(MIX, 0)
     load_first.wait()
     result_in.wait()
     result_out.start()
@@ -1269,8 +1293,6 @@
             query_grads.append(jnp.concatenate(query_parts, 0))
             key_grads.append(tn(query, score_grad[h]))
             value_grads.append(tn(scaled, expon[slot, h]))
-            if h == 0:
-                after("attend", p, 0, 2)
         query_grad = (jnp.where(low, query_grads[0], query_grads[1]) * (1.0 / math.sqrt(half))).astype(BF)
         key_grad = jnp.concatenate([key_grads[0][:half], key_grads[1][half:]], 0).T.astype(BF)
         value_grad = jnp.concatenate([value_grads[0][:half], value_grads[1][half:]], 0).T.astype(BF)
@@ -1296,7 +1318,7 @@
         def _():
             hand(*qkv_chunk(p // 2)).start()
 
-        after("attend", p, 1, 2)
+        after(ATTEND, p)
 
     pl.loop(0, pairs)(attend)
     load_x = pltpu.make_async_copy(i_x, expon.at[0, 0, :, pl.ds(0, width)], local_sems.at[2])
@@ -1307,8 +1329,7 @@
     def close(step):
         source = place.mate(sources - 1 - step)
         at = pl.ds(pl.multiple_of(source * span, span), span)
-        turned = jnp.transpose(code[source])
-        flags = jnp.concatenate([turned[:, 0:1], turned[:, 1:2]], 0) == 1.0
+        flags = column_of(flags_all, source, place.tm) == 1.0
         start = jnp.where(flags, vectors[0:1, :], expon[0, 0, at, 0:width].astype(F32))
         center, speed = moments(start)
         normed = center * speed
@@ -1329,7 +1350,7 @@
                 (place.batch, source),
             ).start()
 
-        after("close", step)
+        after(CLOSE, step)
 
     pl.loop(0, sources)(close)
     own_patch = pltpu.make_async_copy(patch.at[sources - 1], o_patch.at[place.tm], local_sems.at[3])
@@ -1359,10 +1380,10 @@
             moves[-1].start()
 
     deliveries = {
-        "down": (f_down, o_down, [(0, 0, part, part)]),
-        "up": (f_up, o_up, [(j * part, j * width, part, part) for j in range(chunks)]),
-        "out": (f_out, o_out, [(0, 0, part, part)]),
-        "qkv": (
+        DOWN: (f_down, o_down, [(0, 0, part, part)]),
+        UP: (f_up, o_up, [(j * part, j * width, part, part) for j in range(chunks)]),
+        OUT: (f_out, o_out, [(0, 0, part, part)]),
+        QKV: (
             f_qkv,
             o_qkv,
             [
@@ -1372,7 +1393,7 @@
             ],
         ),
     }
-    run(BACKWARD_STEPS["tail"][0])
+    after(TAIL, 0)
     own_small = pltpu.make_async_copy(small.at[4], o_small, local_sems.at[4])
     own_small.start()
     for move in moves:
@@ -1398,7 +1419,7 @@
     shape = jax.ShapeDtypeStruct
     plane = (rows, width)
     small = saved[4]
-    code = saved[7]
+    flags = saved[7]
     halves = [(2 * chips * s.shape[0], s.shape[1] // 2) for s in shards]
     outs = [shape(s.shape, F32) for s in shards] + [shape(small.shape, F32)] + [shape(cotangent.shape, BF)] * 2
     scratch = [
@@ -1422,7 +1443,7 @@
     scratch += [pltpu.VMEM((2 * s.shape[0], s.shape[1] // 2), F32) for s in shards]
     scratch += [
         pltpu.VMEM(small.shape, F32),
-        pltpu.VMEM(code.shape, F32),
+        pltpu.VMEM(flags.shape, jnp.int32),
         pltpu.VMEM((5,) + small.shape, F32),
         pltpu.VMEM((2 + deep,) + small.shape, F32),
         pltpu.VMEM(cotangent.shape, BF),
@@ -1476,11 +1497,8 @@
 ):
     sources, span, width = patches.shape
     shards = (qkv_weight, out_weight, up_weight, down_weight)
-    lane = 128
-    code = jnp.concatenate([mask_flags.reshape(sources, -1, lane), segment_ids.reshape(sources, -1, lane)], 1)
-    code = jnp.pad(code.astype(F32), ((0, 0), (0, 8 - code.shape[1]), (0, 0)))
-    vector = gather_vectors(mask_embed, norm_gain, norm_shift, qv_bias, branch_bias, up_bias)
-    saved = forward(deep, patches, cotangent, code, vector, *shards)
+    vectors = (mask_embed[None], norm_gain, norm_shift, qv_bias, branch_bias, up_bias[None])
+    saved = forward(deep, patches, cotangent, mask_flags, segment_ids, vectors, shards)
     *grads, sums, patch_grad, result = backward(deep, saved, shards, cotangent)
     device = lax.axis_index("batch") * 4 + lax.axis_index("tm")
     piece = mask_embed.shape[0]

time: 244 us -> 242 us (level)
  local copies, waits for them, and re-layouts: 11.1 us -> 6.88 us
where the time goes in v3:
time: 242 us; the launch traced here: 238 us
  Pallas kernels  225 us (93%)
  local copies, waits for them, and re-layouts  6.88 us (3%)
  other arithmetic  5.38 us (2%)
    pallas_call x1, Pallas kernels, backward(): pl.pallas_call(functools.partial(backward_kernel, deep), out_shape=outs,...  117 us
    pallas_call x1, Pallas kernels, forward(): pl.pallas_call(functools.partial(forward_kernel, deep), out_shape=outs, i...  108 us

profile of v3, /device:TPU:11, one launch (start us, length us, event | category | flops | bytes accessed | tf_op | source)
XLA Modules:
  0.0 237.7 jit_solution(10387805273518453308)
XLA Ops:
  0.6 107.9 %forward.1 = (bf16[768,2304]{1,0:T(8,128)(2,1)}, bf16[768,768]{1,0:T(8,128)(2,1)}, bf16[768,3072]{1,0:T(8,128)(2,1)}, bf16[3072,768]{1,0:T(8,128)(2,1)}, f32[16,...) custom-call(bf16[4,256,768]{2,1,0:T(8,128)(2,1)} %patches.1, ...), custom_call_target="tpu_custom_call" | custom-call | tf_op jit(solution)/shard_map/forward/pallas_call | solution.py:835
  108.5 116.9 %backward.1 = (f32[24,2304]{1,0:T(8,128)}, f32[24,768]{1,0:T(8,128)}, f32[24,3072]{1,0:T(8,128)}, f32[96,768]{1,0:T(8,128)}, f32[16,768]{1,0:T(8,128)}, /*index=...) custom-call(bf16[768,2304]{1,0:T(8,128)(2,1)} %get-tuple-element.39.i_qkv, bf16[768,768]{1,0:T(8,128)(2,1)} %get-tuple-element.40.i_out, ...), custom_call_target="tpu_custom_call" | custom-call | tf_op jit(solution)/shard_map/backward/pallas_call | solution.py:1468
  225.4 0.0 copy-start
  225.4 3.5 %convert_element_type.6 = f32[4,256,768]{2,1,0:T(8,128)} convert(bf16[4,256,768]{2,1,0:T(8,128)(2,1)} %get-tuple-element.59) | non-fusion elementwise | flops 786432 | bytes 4718592 | tf_op jit(solution)/shard_map/convert_element_type | solution.py:1508
  228.9 0.0 copy-done
  228.9 0.0 copy-start.3
  228.9 0.0 copy-start.4
  228.9 0.0 copy-start.2
  228.9 0.0 copy-start.1
  228.9 1.9 convert_element_type.7
  230.9 0.7 slice.23
  231.6 0.6 dynamic_slice.7
  232.2 1.5 fusion
  233.7 1.3 dynamic-slice_bitcast_fusion
  235.0 0.0 copy-done.3
  235.0 0.7 copy.30
  235.7 0.0 copy-done.4
  235.7 0.6 copy.31
  236.3 0.0 copy-done.2
  236.3 0.7 copy.32
  237.0 0.0 copy-done.1
  237.0 0.7 copy.33
  (1 shorter events, 0.0 us)
Async XLA Ops:
  225.4 3.5 %copy-start = (bf16[4,256,768]{2,1,0:T(8,128)(2,1)S(1)}, bf16[4,256,768]{2,1,0:T(8,128)(2,1)}, u32[]{:S(2)}) copy-start(bf16[4,256,768]{2,1,0:T(8,128)(2,1)} %get-tuple-element.60) | copy-start | bytes 4718596
  228.9 6.1 %copy-start.3 = (f32[24,2304]{1,0:T(8,128)S(1)}, f32[24,2304]{1,0:T(8,128)}, u32[]{:S(2)}) copy-start(f32[24,2304]{1,0:T(8,128)} %get-tuple-element.87) | copy-start | bytes 663556
  228.9 6.8 %copy-start.4 = (f32[24,768]{1,0:T(8,128)S(1)}, f32[24,768]{1,0:T(8,128)}, u32[]{:S(2)}) copy-start(f32[24,768]{1,0:T(8,128)} %get-tuple-element.89) | copy-start | bytes 221188
  228.9 7.4 %copy-start.2 = (f32[24,3072]{1,0:T(8,128)S(1)}, f32[24,3072]{1,0:T(8,128)}, u32[]{:S(2)}) copy-start(f32[24,3072]{1,0:T(8,128)} %get-tuple-element.91) | copy-start | bytes 884740
  228.9 8.1 %copy-start.1 = (f32[96,768]{1,0:T(8,128)S(1)}, f32[96,768]{1,0:T(8,128)}, u32[]{:S(2)}) copy-start(f32[96,768]{1,0:T(8,128)} %get-tuple-element.93) | copy-start | bytes 884740

commit v4 on v3

--- a/solution.py
+++ b/solution.py
@@ -38,55 +38,55 @@
         0: [
             (FIRST, VECTOR),
             (FIRST, QKV),
+            (FIRST, UP),
             (STAGE, VECTOR, 0, 0, 3),
             (FIRST, OUT),
-            (FIRST, UP),
+            (STAGE, VECTOR, 1, 0, 4),
             (STAGE, QKV, 0, 0, 3),
-            (STAGE, VECTOR, 1, 0, 4),
-            (STAGE, QKV, 1, 0, 4),
-            (ROWS,),
             (STAGE, VECTOR, 2, 0, 8),
             (FINISH, VECTOR),
+            (ROWS,),
+            (STAGE, QKV, 1, 0, 4),
             (STAGE, QKV, 2, 0, 4),
-            (STAGE, OUT, 0, 0, 3),
+            (SPREAD,),
             (STAGE, QKV, 2, 4, 8),
-            (SPREAD,),
-            (FIRST, DOWN),
             (FINISH, QKV),
+            (STAGE, UP, 0, 0, 3),
         ],
     },
     PROJECT: {
         1: [
-            (STAGE, UP, 0, 0, 3),
+            (FIRST, DOWN),
+        ],
+        3: [
+            (STAGE, OUT, 0, 0, 3),
         ],
     },
     ATTEND: {
-        0: [
-            (STAGE, OUT, 1, 0, 4),
-        ],
         1: [
             (STAGE, UP, 1, 0, 4),
+        ],
+        2: [
+            (STAGE, OUT, 1, 0, 4),
             (STAGE, DOWN, 0, 0, 1),
         ],
         3: [
+            (STAGE, UP, 2, 0, 4),
             (STAGE, DOWN, 1, 0, 3),
+        ],
+        5: [
             (STAGE, OUT, 2, 0, 4),
-        ],
-        4: [
-            (STAGE, UP, 2, 0, 4),
             (STAGE, OUT, 2, 4, 8),
             (STAGE, UP, 2, 4, 8),
-        ],
-        5: [
+            (FINISH, OUT),
             (FINISH, UP),
-            (FINISH, OUT),
             (STAGE, DOWN, 1, 3, 6),
         ],
     },
     RISE: {
         0: [
+            (STAGE, DOWN, 2, 0, 4),
             (COTANGENT,),
-            (STAGE, DOWN, 2, 0, 4),
         ],
         1: [
             (STAGE, DOWN, 2, 4, 8),
@@ -126,9 +126,11 @@
         ],
     },
     ATTEND: {
+        0: [
+            (SETTLE, OUT, 0),
+        ],
         1: [
             (ADD, UP, 2, 0),
-            (SETTLE, OUT, 0),
             (ADD, UP, 2, 2),
             (ADD, UP, 2, 3),
         ],
@@ -168,17 +170,17 @@
             (VECTOR_ADD, 0),
             (ADD, UP, 0, 3),
             (SETTLE, QKV, 2),
-            (ADD, QKV, 2, 2),
             (VECTOR_SEND, 1),
             (ADD, UP, 0, 0),
+            (ADD, QKV, 2, 2),
             (ADD, QKV, 1, 0),
             (DELIVER, DOWN),
             (VECTOR_ADD, 1),
             (VECTOR_SEND, 2),
             (VECTOR_ADD, 2),
+            (ADD, QKV, 1, 1),
             (VECTOR_SEND, 3),
             (ADD, QKV, 1, 2),
-            (ADD, QKV, 1, 1),
             (ADD, QKV, 0, 2),
             (ADD, QKV, 0, 0),
             (DELIVER, UP),
@@ -591,8 +593,8 @@
         (
             (VECTOR, zpq, shard_vector, j_vector, w_vector),
             (QKV, zxy, shard_qkv, j_qkv, w_qkv),
-            (OUT, zxy, shard_out, j_out, w_out),
-            (UP, zpq, shard_up, j_up, w_up),
+            (OUT, zpq, shard_out, j_out, w_out),
+            (UP, zxy, shard_up, j_up, w_up),
             (DOWN, pzq, shard_down, j_down, w_down),
         )
     ):
@@ -1212,16 +1214,11 @@
         hand(*up_chunk(j)).start()
         grown = nt(pre_grad, w_up[slot])
 
-        @pl.when(j == 0)
-        def _():
-            gathered[...] = grown
-
-        @pl.when(j > 0)
-        def _():
-            gathered[...] = gathered[...] + grown
+        gathered[...] = gathered[...] + grown
 
         after(FEED, j)
 
+    gathered[...] = jnp.zeros_like(gathered)
     pl.loop(0, chunks)(feed)
     whole_mixed = pltpu.make_async_copy(i_mixed, expon.at[1, 1, :, pl.ds(0, width)], local_sems.at[0])
     whole_mixed.start()
@@ -1306,13 +1303,7 @@
         )
         grown = nt(grads, weight)
 
-        @pl.when(p == 0)
-        def _():
-            first_grad[...] = grown
-
-        @pl.when(p > 0)
-        def _():
-            first_grad[...] = first_grad[...] + grown
+        first_grad[...] = first_grad[...] + grown
 
         @pl.when(p % 2 == 1)
         def _():
@@ -1320,6 +1311,7 @@
 
         after(ATTEND, p)
 
+    first_grad[...] = jnp.zeros_like(first_grad)
     pl.loop(0, pairs)(attend)
     load_x = pltpu.make_async_copy(i_x, expon.at[0, 0, :, pl.ds(0, width)], local_sems.at[2])
     load_x.start()
@@ -1478,6 +1470,52 @@
     )(*saved, cotangent)
 
 
+def finish_kernel(result, patch, sums, *refs):
+    grads, outs = refs[:4], refs[4:]
+    o_result, o_patch, embed, gain, shift, g_qkv, qv, g_out, branch, g_up, up, g_down = outs
+    o_result[...] = result[...].astype(F32)
+    o_patch[...] = patch[...].astype(F32)
+
+    @pl.when(pl.program_id(0) == 0)
+    def _():
+        device = lax.axis_index("batch") * 4 + lax.axis_index("tm")
+        width = sums.shape[1]
+        piece, up_piece = embed.shape[1], up.shape[1]
+        own = pltpu.roll(sums[...], lax.rem(width - device * piece, width), 1)
+        row = 0
+        for out in (embed, gain, shift, qv, branch):
+            out[...] = own[row : row + out.shape[0], :piece]
+            row += out.shape[0]
+        lines = width // up_piece
+        line = jnp.broadcast_to(sums[pl.ds(row + device // lines, 1), :], (8, width))
+        at = lax.rem(width - lax.rem(device, lines) * up_piece, width)
+        up[...] = pltpu.roll(line, at, 1)[0:1, :up_piece]
+        for grad, out in zip(grads, (g_qkv, g_out, g_up, g_down)):
+            out[...] = grad[...]
+
+
+def finish(result, patch_grad, sums, grads, parts):
+    sources, span, width = result.shape
+    shape = jax.ShapeDtypeStruct
+    rows = pl.BlockSpec((2, span, width), lambda i: (i, 0, 0))
+
+    def whole(array):
+        return pl.BlockSpec(array.shape, lambda i: (0, 0))
+
+    vectors = [shape(p.shape, F32) for p in parts]
+    embed, gain, shift, qv, branch, up = vectors
+    outs = [embed, gain, shift, grads[0], qv, grads[1], branch, grads[2], up, grads[3]]
+    outs = [shape(o.shape, F32) for o in outs]
+    return pl.pallas_call(
+        finish_kernel,
+        grid=(sources // 2,),
+        out_shape=[shape(result.shape, F32)] * 2 + outs,
+        in_specs=[rows, rows, whole(sums)] + [whole(g) for g in grads],
+        out_specs=[rows, rows] + [whole(o) for o in outs],
+        name="finish",
+    )(result, patch_grad, sums, *grads)
+
+
 def by_rows(
     deep,
     patches,
@@ -1500,24 +1538,10 @@
     vectors = (mask_embed[None], norm_gain, norm_shift, qv_bias, branch_bias, up_bias[None])
     saved = forward(deep, patches, cotangent, mask_flags, segment_ids, vectors, shards)
     *grads, sums, patch_grad, result = backward(deep, saved, shards, cotangent)
-    device = lax.axis_index("batch") * 4 + lax.axis_index("tm")
-    piece = mask_embed.shape[0]
-    own = lax.dynamic_slice(sums, (0, device * piece), (9, piece))
-    up_sum = lax.dynamic_slice(sums[9:13].reshape(-1), (device * up_bias.shape[0],), up_bias.shape)
-    return (
-        result.astype(F32),
-        patch_grad.astype(F32),
-        own[0],
-        own[1:3],
-        own[3:5],
-        grads[0],
-        own[5:7],
-        grads[1],
-        own[7:9],
-        grads[2],
-        up_sum,
-        grads[3],
+    result, patch_grad, embed, gain, shift, g_qkv, qv, g_out, branch, g_up, up, g_down = finish(
+        result, patch_grad, sums, grads, vectors
     )
+    return result, patch_grad, embed[0], gain, shift, g_qkv, qv, g_out, branch, g_up, up[0], g_down
 
 
 def layer_norm(hidden, gain, shift):

time: 242 us -> 226 us (0.934); the launches traced: 238 us -> 226 us
  local copies, waits for them, and re-layouts: 6.88 us -> 0 us
  other arithmetic: 5.38 us -> 0 us
    pallas_call x1, Pallas kernels: 108 us -> 102 us  [forward(): pl.pallas_call(functools.partial(forward_kernel, deep), out_shape=outs, i...]
    convert_element_type x2 -> x0, other arithmetic: 5.38 us -> none  [the longest x1 3.45 us: by_rows(): result.astype(F32)]
    pallas_call x0 -> x1, Pallas kernels: none -> 4.95 us  [finish(): pl.pallas_call(finish_kernel, grid=(sources // 2,), out_shape=[shape(resu...]
    unnamed x14 -> x0, local copies, waits for them, and re-layouts: 2.76 us -> none
where the time goes in v4:
time: 226 us
  Pallas kernels  225 us (100%)
    pallas_call x1, Pallas kernels, backward(): pl.pallas_call(functools.partial(backward_kernel, deep), out_shape=outs,...  118 us
    pallas_call x1, Pallas kernels, forward(): pl.pallas_call(functools.partial(forward_kernel, deep), out_shape=outs, i...  102 us
    pallas_call x1, Pallas kernels, finish(): pl.pallas_call(finish_kernel, grid=(sources // 2,), out_shape=[shape(resu...  4.95 us

profile of v4, /device:TPU:11, one launch (start us, length us, event | category | flops | bytes accessed | tf_op | source)
XLA Modules:
  0.0 226.0 jit_solution(9353306503680558654)
XLA Ops:
  0.6 102.0 %forward.1 = (bf16[768,2304]{1,0:T(8,128)(2,1)}, bf16[768,768]{1,0:T(8,128)(2,1)}, bf16[768,3072]{1,0:T(8,128)(2,1)}, bf16[3072,768]{1,0:T(8,128)(2,1)}, f32[16,...) custom-call(bf16[4,256,768]{2,1,0:T(8,128)(2,1)} %patches.1, ...), custom_call_target="tpu_custom_call" | custom-call | tf_op jit(solution)/shard_map/forward/pallas_call | solution.py:837
  102.7 118.2 %backward.1 = (f32[24,2304]{1,0:T(8,128)}, f32[24,768]{1,0:T(8,128)}, f32[24,3072]{1,0:T(8,128)}, f32[96,768]{1,0:T(8,128)}, f32[16,768]{1,0:T(8,128)}, /*index=...) custom-call(bf16[768,2304]{1,0:T(8,128)(2,1)} %get-tuple-element.51.i_qkv, bf16[768,768]{1,0:T(8,128)(2,1)} %get-tuple-element.52.i_out, ...), custom_call_target="tpu_custom_call" | custom-call | tf_op jit(solution)/shard_map/backward/pallas_call | solution.py:1460
  220.9 4.9 %finish.1 = (f32[4,256,768]{2,1,0:T(8,128)}, f32[4,256,768]{2,1,0:T(8,128)}, f32[1,24]{1,0:T(1,128)}, f32[2,24]{1,0:T(2,128)}, f32[2,24]{1,0:T(2,128)}, /*index=...) custom-call(bf16[4,256,768]{2,1,0:T(8,128)(2,1)} %get-tuple-element., ...), custom_call_target="tpu_custom_call" | custom-call | tf_op jit(solution)/shard_map/finish/pallas_call | solution.py:1509

commit v5 on v4

--- a/solution.py
+++ b/solution.py
@@ -1476,28 +1476,26 @@
     o_result[...] = result[...].astype(F32)
     o_patch[...] = patch[...].astype(F32)
 
-    @pl.when(pl.program_id(0) == 0)
-    def _():
-        device = lax.axis_index("batch") * 4 + lax.axis_index("tm")
-        width = sums.shape[1]
-        piece, up_piece = embed.shape[1], up.shape[1]
-        own = pltpu.roll(sums[...], lax.rem(width - device * piece, width), 1)
-        row = 0
-        for out in (embed, gain, shift, qv, branch):
-            out[...] = own[row : row + out.shape[0], :piece]
-            row += out.shape[0]
-        lines = width // up_piece
-        line = jnp.broadcast_to(sums[pl.ds(row + device // lines, 1), :], (8, width))
-        at = lax.rem(width - lax.rem(device, lines) * up_piece, width)
-        up[...] = pltpu.roll(line, at, 1)[0:1, :up_piece]
-        for grad, out in zip(grads, (g_qkv, g_out, g_up, g_down)):
-            out[...] = grad[...]
+    for grad, out in zip(grads, (g_qkv, g_out, g_up, g_down)):
+        out[...] = grad[...]
+
+    device = lax.axis_index("batch") * 4 + lax.axis_index("tm")
+    width = sums.shape[1]
+    piece, up_piece = embed.shape[1], up.shape[1]
+    own = pltpu.roll(sums[...], lax.rem(width - device * piece, width), 1)
+    row = 0
+    for out in (embed, gain, shift, qv, branch):
+        out[...] = own[row : row + out.shape[0], :piece]
+        row += out.shape[0]
+    lines = width // up_piece
+    line = jnp.broadcast_to(sums[pl.ds(row + device // lines, 1), :], (8, width))
+    at = lax.rem(width - lax.rem(device, lines) * up_piece, width)
+    up[...] = pltpu.roll(line, at, 1)[0:1, :up_piece]
 
 
 def finish(result, patch_grad, sums, grads, parts):
-    sources, span, width = result.shape
     shape = jax.ShapeDtypeStruct
-    rows = pl.BlockSpec((2, span, width), lambda i: (i, 0, 0))
+    rows = pl.BlockSpec(result.shape, lambda i: (0, 0, 0))
 
     def whole(array):
         return pl.BlockSpec(array.shape, lambda i: (0, 0))
@@ -1508,10 +1506,11 @@
     outs = [shape(o.shape, F32) for o in outs]
     return pl.pallas_call(
         finish_kernel,
-        grid=(sources // 2,),
+        grid=(1,),
         out_shape=[shape(result.shape, F32)] * 2 + outs,
         in_specs=[rows, rows, whole(sums)] + [whole(g) for g in grads],
         out_specs=[rows, rows] + [whole(o) for o in outs],
+        compiler_params=pltpu.CompilerParams(vmem_limit_bytes=40 * 2**20),
         name="finish",
     )(result, patch_grad, sums, *grads)
 

time: 226 us -> 232 us (1.027)
  local copies, waits for them, and re-layouts: 0 us -> 7.35 us
    unnamed x0 -> x14, local copies, waits for them, and re-layouts: none -> 7.35 us
where the time goes in v5:
time: 232 us; the launch traced here: 231 us
  Pallas kernels  223 us (96%)
  local copies, waits for them, and re-layouts  7.35 us (3%)
    pallas_call x1, Pallas kernels, backward(): pl.pallas_call(functools.partial(backward_kernel, deep), out_shape=outs,...  118 us
    pallas_call x1, Pallas kernels, forward(): pl.pallas_call(functools.partial(forward_kernel, deep), out_shape=outs, i...  102 us
    unnamed x14, local copies, waits for them, and re-layouts  7.35 us

profile of v5, /device:TPU:11, one launch (start us, length us, event | category | flops | bytes accessed | tf_op | source)
XLA Modules:
  0.0 231.5 jit_solution(11195397395850077843)
XLA Ops:
  0.6 102.0 %forward.1 = (bf16[768,2304]{1,0:T(8,128)(2,1)}, bf16[768,768]{1,0:T(8,128)(2,1)}, bf16[768,3072]{1,0:T(8,128)(2,1)}, bf16[3072,768]{1,0:T(8,128)(2,1)}, f32[16,...) custom-call(bf16[4,256,768]{2,1,0:T(8,128)(2,1)} %patches.1, ...), custom_call_target="tpu_custom_call" | custom-call | tf_op jit(solution)/shard_map/forward/pallas_call | solution.py:837
  102.7 118.1 %backward.1 = (f32[24,2304]{1,0:T(8,128)}, f32[24,768]{1,0:T(8,128)}, f32[24,3072]{1,0:T(8,128)}, f32[96,768]{1,0:T(8,128)}, f32[16,768]{1,0:T(8,128)}, /*index=...) custom-call(bf16[768,2304]{1,0:T(8,128)(2,1)} %get-tuple-element.51.i_qkv, bf16[768,768]{1,0:T(8,128)(2,1)} %get-tuple-element.52.i_out, ...), custom_call_target="tpu_custom_call" | custom-call | tf_op jit(solution)/shard_map/backward/pallas_call | solution.py:1460
  220.8 0.0 copy-start
  220.8 1.4 copy-done
  222.2 0.0 copy-start.1
  222.2 1.4 copy-done.1
  223.6 0.0 copy-start.2
  223.6 1.0 copy-done.2
  224.5 0.0 copy-start.3
  224.5 1.0 copy-done.3
  225.5 0.0 copy-start.4
  225.5 0.9 copy-done.4
  226.4 0.0 copy-start.5
  226.4 0.9 copy-done.5
  227.3 0.0 copy-start.6
  227.3 0.8 copy-done.6
  228.1 3.2 %finish.1 = (f32[4,256,768]{2,1,0:T(8,128)}, f32[4,256,768]{2,1,0:T(8,128)}, f32[1,24]{1,0:T(1,128)}, f32[2,24]{1,0:T(2,128)}, f32[2,24]{1,0:T(2,128)}, /*index=...) custom-call(bf16[4,256,768]{2,1,0:T(8,128)(2,1)S(1)} %copy-done.1, ...), custom_call_target="tpu_custom_call" | custom-call | tf_op jit(solution)/shard_map/finish/pallas_call | solution.py:1507
Async XLA Ops:
  220.8 1.4 copy-start
  222.2 1.4 copy-start.1
  223.6 1.0 copy-start.2
  224.5 1.0 copy-start.3
  225.5 0.9 copy-start.4
  226.4 0.9 copy-start.5
  227.3 0.8 copy-start.6

commit v6 on v4

--- a/solution.py
+++ b/solution.py
@@ -1270,6 +1270,8 @@
             for copy in pair_loads(p + 1):
                 copy.start()
 
+        pl.when(p == pairs - 1)(lambda: load_x.start())
+
         for copy in pair_loads(p):
             copy.wait()
         scaled = (mixed_grad[:, lanes].astype(F32) * rate[slot]).astype(BF)
@@ -1311,10 +1313,9 @@
 
         after(ATTEND, p)
 
+    load_x = pltpu.make_async_copy(i_x, expon.at[0, 0, :, pl.ds(0, width)], local_sems.at[2])
     first_grad[...] = jnp.zeros_like(first_grad)
     pl.loop(0, pairs)(attend)
-    load_x = pltpu.make_async_copy(i_x, expon.at[0, 0, :, pl.ds(0, width)], local_sems.at[2])
-    load_x.start()
     load_x.wait()
     result_out.wait()
 

time: 226 us -> 227 us (level)
  no operation moved by 1% of the time
where the time goes in v6:
time: 227 us
  Pallas kernels  226 us (100%)
    pallas_call x1, Pallas kernels, backward(): pl.pallas_call(functools.partial(backward_kernel, deep), out_shape=outs,...  119 us
    pallas_call x1, Pallas kernels, forward(): pl.pallas_call(functools.partial(forward_kernel, deep), out_shape=outs, i...  102 us
    pallas_call x1, Pallas kernels, finish(): pl.pallas_call(finish_kernel, grid=(sources // 2,), out_shape=[shape(resu...  4.95 us

profile of v6, /device:TPU:11, one launch (start us, length us, event | category | flops | bytes accessed | tf_op | source)
XLA Modules:
  0.0 226.8 jit_solution(370830050446610455)
XLA Ops:
  0.6 102.0 %forward.1 = (bf16[768,2304]{1,0:T(8,128)(2,1)}, bf16[768,768]{1,0:T(8,128)(2,1)}, bf16[768,3072]{1,0:T(8,128)(2,1)}, bf16[3072,768]{1,0:T(8,128)(2,1)}, f32[16,...) custom-call(bf16[4,256,768]{2,1,0:T(8,128)(2,1)} %patches.1, ...), custom_call_target="tpu_custom_call" | custom-call | tf_op jit(solution)/shard_map/forward/pallas_call | solution.py:837
  102.7 119.0 %backward.1 = (f32[24,2304]{1,0:T(8,128)}, f32[24,768]{1,0:T(8,128)}, f32[24,3072]{1,0:T(8,128)}, f32[96,768]{1,0:T(8,128)}, f32[16,768]{1,0:T(8,128)}, /*index=...) custom-call(bf16[768,2304]{1,0:T(8,128)(2,1)} %get-tuple-element.51.i_qkv, bf16[768,768]{1,0:T(8,128)(2,1)} %get-tuple-element.52.i_out, ...), custom_call_target="tpu_custom_call" | custom-call | tf_op jit(solution)/shard_map/backward/pallas_call | solution.py:1461
  221.7 4.9 %finish.1 = (f32[4,256,768]{2,1,0:T(8,128)}, f32[4,256,768]{2,1,0:T(8,128)}, f32[1,24]{1,0:T(1,128)}, f32[2,24]{1,0:T(2,128)}, f32[2,24]{1,0:T(2,128)}, /*index=...) custom-call(bf16[4,256,768]{2,1,0:T(8,128)(2,1)} %get-tuple-element., ...), custom_call_target="tpu_custom_call" | custom-call | tf_op jit(solution)/shard_map/finish/pallas_call | solution.py:1510
